TPU v7x, 256 devices: a whole 4x4x8 slice. The times are simulated.
256 devices in a mesh: dp: 32 (over z, y), tensor: 8 (over x, core).
Axes of the slice: x: 4, y: 4, z: 8, core: 2. Of those that a mesh axis runs over, the one named last changes fastest.
Arguments:
- hidden: bfloat16 [1024, 48, 8192], P('dp'), may hold values from -6 to 6
- norm_gain: bfloat16 [8192], replicated, may hold values from 0.099609375 to 1.8984375
- kv_weight: bfloat16 [2048, 8192], P('tensor', 'dp')
- lengths: int32 [1024], P('dp'), may hold values from 1 to 48, as said below
- owner: int32 [1024], P('dp'), may hold values from 0 to 31, as said below
Outputs:
- kv_cache: bfloat16 [1024, 48, 2048], P(('dp', 'tensor'))
Inputs may be any that keep to these rules, and one draw needn't show every extreme that they name: Within the 32 sequences of one dp index every owner appears exactly once. `lengths`: some sequence has length 1 and some has length 48.
All inputs are finite; a program needn't handle non-finite values.
Results may differ from a plain program's by a relative error of at most 0.0053.
Values may be sent and summed in bfloat16 or wider, within the bound.
No kernel may reach another device: no remote copies, remote signals or barrier semaphores. Data moves between devices by JAX's collectives and lax.ppermute only.
A program may use at most 128 MiB of HBM per device.

v0:
```python
import functools

import jax
import jax.numpy as jnp
from jax import lax
from jax.experimental import pallas as pl
from jax.experimental.pallas import tpu as pltpu
from jax.sharding import Mesh
from jax.sharding import PartitionSpec as P

HD = 128
EPSILON = 1e-05
WEIGHT_EPSILON = 1e-12
SATURATION = 2.0
ROPE_BASE = 500000.0
NZ, NY = 8, 4
PER_STEP = 8
VMEM_LIMIT = 40 * 1024 * 1024


def from_z(value, step):
    return lax.ppermute(value, "z", [((s + step) % NZ, s) for s in range(NZ)])


def from_y(value, step):
    return lax.ppermute(value, "y", [((s + step) % NY, s) for s in range(NY)])


def gather_y_then_z(own):
    up, down, far = from_y(own, 1), from_y(own, -1), from_y(own, 2)
    pair, rest = jnp.concatenate([own, up], axis=0), jnp.concatenate([down, far], axis=0)
    dys, others = [0, 1], [-1, 2]
    pieces = [(pair, [(0, dy) for dy in dys]), (rest, [(0, dy) for dy in others])]
    pair_up = pair_down = pair
    rest_up = rest_down = rest
    for s in range(1, 4):
        pair_up, pair_down = from_z(pair_up, 1), from_z(pair_down, -1)
        rest_up, rest_down = from_z(rest_up, 1), from_z(rest_down, -1)
        pieces += [(pair_up, [(s, dy) for dy in dys]), (pair_down, [(-s, dy) for dy in dys])]
        pieces += [(rest_up, [(s, dy) for dy in others]), (rest_down, [(-s, dy) for dy in others])]
    pieces.append((from_z(pair_up, 1), [(4, dy) for dy in dys]))
    pieces.append((from_z(rest_down, -1), [(4, dy) for dy in others]))
    return pieces


def gather_z_then_y(own):
    up1, down1 = from_z(own, 1), from_z(own, -1)
    up2, down2 = from_z(own, 2), from_z(own, -2)
    near, near_dz = jnp.concatenate([own, up1, down1, up2], axis=0), [0, 1, -1, 2]
    near_up, near_down = from_y(near, 1), from_y(near, -1)
    up3, down3, up4 = from_z(up2, 1), from_z(down2, -1), from_z(up2, 2)
    late, late_dz = jnp.concatenate([down2, up3, down3, up4], axis=0), [-2, 3, -3, 4]
    late_up, late_down = from_y(late, 1), from_y(late, -1)
    pieces = []
    for array, dzs, dy in (
        (near, near_dz, 0),
        (late, late_dz, 0),
        (near_up, near_dz, 1),
        (near_down, near_dz, -1),
        (late_up, late_dz, 1),
        (late_down, late_dz, -1),
        (from_y(near_up, 1), near_dz, 2),
        (from_y(late_down, -1), late_dz, 2),
    ):
        pieces.append((array, [(dz, dy) for dz in dzs]))
    return pieces


def write_codes(meta, place_ref, gain_ref, piece_refs, out_ref):
    z, y = place_ref[0], place_ref[1]
    rows, width = out_ref.shape
    blocks = [(ref, n, dz, dy) for ref, offsets in zip(piece_refs, meta) for n, (dz, dy) in enumerate(offsets)]
    cols = piece_refs[0].shape[2]
    total = jnp.zeros((rows, HD), jnp.float32)
    for ref, n, _, _ in blocks:
        for c in range(0, cols, HD):
            wide = ref[n, :, c : c + HD].astype(jnp.float32)
            total += wide * wide
    squares = jnp.sum(total, axis=1, keepdims=True)
    threshold = SATURATION * jnp.sqrt(squares / width + WEIGHT_EPSILON)
    high = jnp.broadcast_to(threshold.astype(jnp.bfloat16), (rows, cols))
    for ref, n, dz, dy in blocks:
        at = (((z + dz + NZ) % NZ) * NY + (y + dy + NY) % NY) * cols
        at = pl.multiple_of(at, cols)
        code = jnp.minimum(jnp.maximum(ref[n], -high), high)
        out_ref[:, pl.ds(at, cols)] = code * gain_ref[:, pl.ds(at, cols)]


def project_kernel(meta, place_ref, slot_ref, length_ref, hidden_ref, cosine_ref, sine_ref, gain_ref, *refs):
    piece_refs, refs = refs[: len(meta)], refs[len(meta) :]
    result_ref, codes_ref = refs
    count, cap, width = hidden_ref.shape
    step = pl.program_id(0)

    @pl.when(step == 0)
    def _():
        write_codes(meta, place_ref, gain_ref, piece_refs, codes_ref)

    raw = lax.dot_general(
        hidden_ref[...].reshape(count * cap, width),
        codes_ref[...],
        (((1,), (1,)), ((), ())),
        preferred_element_type=jnp.float32,
    )
    position = lax.broadcasted_iota(jnp.int32, (cap, HD), 0)
    for j in range(count):
        squares = jnp.zeros((cap, HD), jnp.float32)
        for c in range(0, width, HD):
            wide = hidden_ref[j, :, c : c + HD].astype(jnp.float32)
            squares += wide * wide
        mean = jnp.sum(squares, axis=1, keepdims=True) / width
        scale = jnp.broadcast_to(lax.rsqrt(mean + EPSILON), (cap, HD))
        sequence = step * count + j
        scale = jnp.where(position < length_ref[sequence], scale, 0.0)
        keys = raw[j * cap : (j + 1) * cap, :HD] * scale
        values = raw[j * cap : (j + 1) * cap, HD:] * scale
        keys = keys * cosine_ref[...] + pltpu.roll(keys, HD // 2, 1) * sine_ref[...]
        slot = slot_ref[sequence]
        result_ref[slot, :, :HD] = keys.astype(jnp.bfloat16)
        result_ref[slot, :, HD:] = values.astype(jnp.bfloat16)


def project(place, slot, lengths, hidden, cosine, sine, pieces, gain):
    seqs, cap, width = hidden.shape
    rows = pieces[0][0].shape[1]
    smem = pl.BlockSpec(memory_space=pltpu.SMEM)
    whole = lambda shape: pl.BlockSpec(shape, lambda i: (0,) * len(shape))
    return pl.pallas_call(
        functools.partial(project_kernel, [m for _, m in pieces]),
        grid=(seqs // PER_STEP,),
        out_shape=jax.ShapeDtypeStruct((seqs, cap, rows), jnp.bfloat16),
        in_specs=[smem] * 3
        + [pl.BlockSpec((PER_STEP, cap, width), lambda i: (i, 0, 0))]
        + [whole(a.shape) for a in (cosine, sine, gain)]
        + [whole(a.shape) for a, _ in pieces],
        out_specs=whole((seqs, cap, rows)),
        scratch_shapes=[pltpu.VMEM((rows, width), jnp.bfloat16)],
        compiler_params=pltpu.CompilerParams(vmem_limit_bytes=VMEM_LIMIT),
        cost_estimate=pl.CostEstimate(
            flops=2 * seqs * cap * width * rows, bytes_accessed=2 * seqs * cap * width, transcendentals=0
        ),
        name="project",
    )(place, slot, lengths, hidden, cosine, sine, gain, *[a for a, _ in pieces])


def run(gather, own, hidden, gain, place, slot, lengths, cosine, sine):
    by_target = project(place, slot, lengths, hidden, cosine, sine, gather(own), gain.reshape(1, -1))
    return lax.all_to_all(by_target, ("z", "y"), split_axis=0, concat_axis=0, tiled=True)


def shards(hidden, norm_gain, kv_weight, lengths, owner):
    _, cap, width = hidden.shape
    rows, cols = kv_weight.shape
    z, y = lax.axis_index("z"), lax.axis_index("y")
    place = jnp.stack([z, y]).astype(jnp.int32)
    own = kv_weight.reshape(1, rows, cols)

    frequency = ROPE_BASE ** (-(2.0 * jnp.arange(HD // 2, dtype=jnp.float32)) / HD)
    angles = jnp.arange(cap, dtype=jnp.float32)[:, None] * frequency[None, :]
    cosine = jnp.concatenate([jnp.cos(angles)] * 2, axis=1)
    sine = jnp.concatenate([-jnp.sin(angles), jnp.sin(angles)], axis=1)

    grouped = lax.cond(
        lax.axis_index("c") == 0,
        functools.partial(run, gather_y_then_z),
        functools.partial(run, gather_z_then_y),
        own, hidden, norm_gain, place, owner, lengths, cosine, sine,
    )
    landed = lax.all_to_all(grouped, ("x", "c"), split_axis=0, concat_axis=0, tiled=True)
    landed = landed.reshape(-1, NY, cap, rows)
    return jnp.transpose(landed, (1, 2, 0, 3)).reshape(NY, cap, -1)


def solution(mesh):
    split = Mesh(mesh.devices.reshape(NZ, NY, 4, 2), ("z", "y", "x", "c"))
    dp, tensor = ("z", "y"), ("x", "c")
    return jax.shard_map(
        shards,
        mesh=split,
        in_specs=(P(dp, None, None), P(), P(tensor, dp), P(dp), P(dp)),
        out_specs=P(("z", "y", "x", "c"), None, None),
        check_vma=False,
    )
```

profile of v0, /device:TPU:1, one launch (start us, length us, event | category | flops | bytes accessed | tf_op | source)
XLA Modules:
  0.0 109.0 jit_solution(12270269605836629263)
XLA Ops:
  0.0 0.1 fusion.2
  0.3 84.3 %conditional.1 = (bf16[32,48,256]{2,1,0:T(8,128)(2,1)S(1)}) conditional(s32[]{:T(128)} %convert_element_type.3, (bf16[8192]{0:T(1024)(128)(2,1)}, bf16[1,256,256]{2,1,0:T(8,128)(2,1)}, s32[2]{0:T(128)S(1)}, s32[32]{0:T(128)}, s32[32]{0:T(128)}, /*index=5*/bf16[32,48,8192]{2,1,0:T(8,128)(2,1)}, f32[48,128]{1,0:T(8,128)S(1)}, ...), branch_computations={%region_0.0_spmd, %region_1.0_spmd} | conditional | flops 6442450944 | bytes 45122064 | solution.py:163
  0.3 6.9 %collective-permute-start.2 = (bf16[1,256,256]{2,1,0:T(8,128)(2,1)}, bf16[1,256,256]{2,1,0:T(8,128)(2,1)S(1)}, u32[]{:S(2)}, u32[]{:S(2)}) collective-permute-start(bf16[1,256,256]{2,1,0:T(8,128)(2,1)} %get-tuple-element.47), channel_id=1, source_target_pairs={{64,0},{96,32},{128,64},{160,96},{192,128},{224,160},{0,192},{32,2... | collective-permute-start | bytes 393224 | tf_op jit(solution)/shard_map/cond/branch_0_fun/ppermute | solution.py:22
  7.2 0.7 collective-permute-start
  8.0 1.2 %collective-permute-start.3 = (bf16[1,256,256]{2,1,0:T(8,128)(2,1)}, bf16[1,256,256]{2,1,0:T(8,128)(2,1)S(1)}, u32[]{:S(2)}, u32[]{:S(2)}) collective-permute-start(bf16[1,256,256]{2,1,0:T(8,128)(2,1)} %get-tuple-element.47), channel_id=1, source_target_pairs={{192,0},{224,32},{0,64},{32,96},{64,128},{96,160},{128,192},{160,2... | collective-permute-start | bytes 393224 | tf_op jit(solution)/shard_map/cond/branch_0_fun/ppermute | solution.py:22
  9.2 1.0 constant_dynamic-update-slice_fusion.3
  10.1 0.8 collective-permute-done.2
  10.9 2.1 %collective-permute-start.4 = (bf16[1,256,256]{2,1,0:T(8,128)(2,1)S(1)}, bf16[1,256,256]{2,1,0:T(8,128)(2,1)S(1)}, u32[]{:S(2)}, u32[]{:S(2)}) collective-permute-start(bf16[1,256,256]{2,1,0:T(8,128)(2,1)S(1)} %collective-permute-done.2), channel_id=1, source_target_pairs={{32,0},{64,32},{96,64},{128,96},{160,128},{192,160},{224,192},{0,2... | collective-permute-start | bytes 393224 | tf_op jit(solution)/shard_map/cond/branch_0_fun/ppermute | solution.py:22
  13.0 3.4 %collective-permute-done.1 = bf16[1,256,256]{2,1,0:T(8,128)(2,1)S(1)} collective-permute-done((bf16[1,256,256]{2,1,0:T(8,128)(2,1)}, bf16[1,256,256]{2,1,0:T(8,128)(2,1)S(1)}, u32[]{:S(2)}, u32[]{:S(2)}) %collective-permute-start.1) | collective-permute-done | bytes 131104 | tf_op jit(solution)/shard_map/cond/branch_0_fun/ppermute | solution.py:22
  16.5 2.8 %collective-permute-start.7 = (bf16[4,256,256]{2,1,0:T(8,128)(2,1)S(1)}, bf16[4,256,256]{2,1,0:T(8,128)(2,1)S(1)}, u32[]{:S(2)}, u32[]{:S(2)}) collective-permute-start(bf16[4,256,256]{2,1,0:T(8,128)(2,1)S(1)} %constant_dynamic-update-slice_fusion.refs_0_), channel_id=1, source_target_pairs={{8,0},{16,8},{24,16},{0,24},{9,1},{17,9},{25,17},{1,25},{10,2},{18... | collective-permute-start | bytes 1572872 | tf_op jit(solution)/shard_map/cond/branch_0_fun/ppermute | solution.py:26
  19.4 1.8 %collective-permute-start.5 = (bf16[1,256,256]{2,1,0:T(8,128)(2,1)S(1)}, bf16[1,256,256]{2,1,0:T(8,128)(2,1)S(1)}, u32[]{:S(2)}, u32[]{:S(2)}) collective-permute-start(bf16[1,256,256]{2,1,0:T(8,128)(2,1)S(1)} %collective-permute-done.3), channel_id=1, source_target_pairs={{224,0},{0,32},{32,64},{64,96},{96,128},{128,160},{160,192},{192,2... | collective-permute-start | bytes 393224 | tf_op jit(solution)/shard_map/cond/branch_0_fun/ppermute | solution.py:22
  21.2 4.9 %collective-permute-done.5 = bf16[1,256,256]{2,1,0:T(8,128)(2,1)S(1)} collective-permute-done((bf16[1,256,256]{2,1,0:T(8,128)(2,1)S(1)}, bf16[1,256,256]{2,1,0:T(8,128)(2,1)S(1)}, u32[]{:S(2)}, u32[]{:S(2)}) %collective-permute-start.5) | collective-permute-done | bytes 131104 | tf_op jit(solution)/shard_map/cond/branch_0_fun/ppermute | solution.py:22
  26.2 0.7 collective-permute-done.6
  27.0 2.7 %collective-permute-start.9 = (bf16[4,256,256]{2,1,0:T(8,128)(2,1)S(1)}, bf16[4,256,256]{2,1,0:T(8,128)(2,1)S(1)}, u32[]{:S(2)}, u32[]{:S(2)}) collective-permute-start(bf16[4,256,256]{2,1,0:T(8,128)(2,1)S(1)} %constant_dynamic-update-slice_fusion.4.refs_1_), channel_id=1, source_target_pairs={{8,0},{16,8},{24,16},{0,24},{9,1},{17,9},{25,17},{1,25},{10,2},{18... | collective-permute-start | bytes 1572872 | tf_op jit(solution)/shard_map/cond/branch_0_fun/ppermute | solution.py:26
  29.7 1.4 %collective-permute-start.11 = (bf16[4,256,256]{2,1,0:T(8,128)(2,1)S(1)}, bf16[4,256,256]{2,1,0:T(8,128)(2,1)S(1)}, u32[]{:S(2)}, u32[]{:S(2)}) collective-permute-start(bf16[4,256,256]{2,1,0:T(8,128)(2,1)S(1)} %collective-permute-done.7.refs_2_), channel_id=1, source_target_pairs={{8,0},{16,8},{24,16},{0,24},{9,1},{17,9},{25,17},{1,25},{10,2},{18... | collective-permute-start | bytes 1572872 | tf_op jit(solution)/shard_map/cond/branch_0_fun/ppermute | solution.py:26
  31.1 5.1 %collective-permute-done.10.refs_5_ = bf16[4,256,256]{2,1,0:T(8,128)(2,1)S(1)} collective-permute-done((bf16[4,256,256]{2,1,0:T(8,128)(2,1)S(1)}, bf16[4,256,256]{2,1,0:T(8,128)(2,1)S(1)}, u32[]{:S(2)}, u32[]{:S(2)}) %collective-permute-start.10) | collective-permute-done | bytes 524320 | tf_op jit(solution)/shard_map/cond/branch_0_fun/ppermute | solution.py:26
  36.2 0.7 reshape.17.gain_ref
  36.9 5.2 %collective-permute-done.8.refs_3_ = bf16[4,256,256]{2,1,0:T(8,128)(2,1)S(1)} collective-permute-done((bf16[4,256,256]{2,1,0:T(8,128)(2,1)S(1)}, bf16[4,256,256]{2,1,0:T(8,128)(2,1)S(1)}, u32[]{:S(2)}, u32[]{:S(2)}) %collective-permute-start.8) | collective-permute-done | bytes 524320 | tf_op jit(solution)/shard_map/cond/branch_0_fun/ppermute | solution.py:26
  42.1 5.6 %collective-permute-done.12.refs_7_ = bf16[4,256,256]{2,1,0:T(8,128)(2,1)S(1)} collective-permute-done((bf16[4,256,256]{2,1,0:T(8,128)(2,1)S(1)}, bf16[4,256,256]{2,1,0:T(8,128)(2,1)S(1)}, u32[]{:S(2)}, u32[]{:S(2)}) %collective-permute-start.12) | collective-permute-done | bytes 524320 | tf_op jit(solution)/shard_map/cond/branch_0_fun/ppermute | solution.py:26
  47.7 16.4 %project.2 = bf16[32,48,256]{2,1,0:T(8,128)(2,1)S(1)} custom-call(s32[2]{0:T(128)S(1)} %get-tuple-element.40.place_ref, s32[32]{0:T(128)} %get-tuple-element.41.slot_ref, s32[32]{0:T(128)} %get-tuple-element.42.length_ref, bf16[32,48,8192]{2,1,0:T(8,128)(2,1)} %get-tuple-element.43.hidden_ref, f32[48,128]{1,0:T(8,128)S(1)} %get-tuple-element.44.cosine_ref, ...), custom_call_target="tpu_custom_call" | custom-call | flops 6442450944 | bytes 25165824 | tf_op jit(solution)/shard_map/cond/branch_0_fun/project/pallas_call | solution.py:128
  64.1 20.5 %all_to_all.13 = bf16[32,48,256]{2,1,0:T(8,128)(2,1)S(1)} all-to-all(bf16[32,48,256]{2,1,0:T(8,128)(2,1)S(1)} %project.2), channel_id=1, replica_groups=mesh['z'=8,'y'=4,'x'=4,'c'=2] {'z','y'}, dimensions={0} | all-to-all | bytes 1572864 | tf_op jit(solution)/shard_map/cond/branch_0_fun/all_to_all | solution.py:148
  84.6 22.7 %all_to_all.15 = bf16[32,48,256]{2,1,0:T(8,128)(2,1)S(1)} all-to-all(bf16[32,48,256]{2,1,0:T(8,128)(2,1)S(1)} %get-tuple-element.61), channel_id=1, replica_groups=mesh['z'=8,'y'=4,'x'=4,'c'=2] {'x','c'}, dimensions={0} | all-to-all | bytes 1572864 | tf_op jit(solution)/shard_map/all_to_all | solution.py:169
  107.3 0.4 copy.8
  107.8 1.2 %reshape.24 = bf16[4,48,2048]{2,1,0:T(8,128)(2,1)} reshape(bf16[4,48,8,256]{3,2,1,0:T(8,128)(2,1)S(1)} %bitcast.10) | data formatting | bytes 1572864 | tf_op jit(solution)/shard_map/reshape | solution.py:171
  (21 shorter events, 0.5 us)
Async XLA Ops:
  0.3 10.6 %collective-permute-start.2 = (bf16[1,256,256]{2,1,0:T(8,128)(2,1)}, bf16[1,256,256]{2,1,0:T(8,128)(2,1)S(1)}, u32[]{:S(2)}, u32[]{:S(2)}) collective-permute-start(bf16[1,256,256]{2,1,0:T(8,128)(2,1)} %get-tuple-element.47), channel_id=1, source_target_pairs={{64,0},{96,32},{128,64},{160,96},{192,128},{224,160},{0,192},{32,2... | collective-permute-start | bytes 393224 | tf_op jit(solution)/shard_map/cond/branch_0_fun/ppermute | solution.py:22
  7.2 5.8 %collective-permute-start = (bf16[1,256,256]{2,1,0:T(8,128)(2,1)}, bf16[1,256,256]{2,1,0:T(8,128)(2,1)S(1)}, u32[]{:S(2)}, u32[]{:S(2)}) collective-permute-start(bf16[1,256,256]{2,1,0:T(8,128)(2,1)} %get-tuple-element.47), channel_id=1, source_target_pairs={{32,0},{64,32},{96,64},{128,96},{160,128},{192,160},{224,192},{0,2... | collective-permute-start | bytes 393224 | tf_op jit(solution)/shard_map/cond/branch_0_fun/ppermute | solution.py:22
  8.0 11.4 %collective-permute-start.3 = (bf16[1,256,256]{2,1,0:T(8,128)(2,1)}, bf16[1,256,256]{2,1,0:T(8,128)(2,1)S(1)}, u32[]{:S(2)}, u32[]{:S(2)}) collective-permute-start(bf16[1,256,256]{2,1,0:T(8,128)(2,1)} %get-tuple-element.47), channel_id=1, source_target_pairs={{192,0},{224,32},{0,64},{32,96},{64,128},{96,160},{128,192},{160,2... | collective-permute-start | bytes 393224 | tf_op jit(solution)/shard_map/cond/branch_0_fun/ppermute | solution.py:22
  9.2 7.3 %collective-permute-start.1 = (bf16[1,256,256]{2,1,0:T(8,128)(2,1)}, bf16[1,256,256]{2,1,0:T(8,128)(2,1)S(1)}, u32[]{:S(2)}, u32[]{:S(2)}) collective-permute-start(bf16[1,256,256]{2,1,0:T(8,128)(2,1)} %get-tuple-element.47), channel_id=1, source_target_pairs={{224,0},{0,32},{32,64},{64,96},{96,128},{128,160},{160,192},{192,2... | collective-permute-start | bytes 393224 | tf_op jit(solution)/shard_map/cond/branch_0_fun/ppermute | solution.py:22
  10.9 10.3 %collective-permute-start.4 = (bf16[1,256,256]{2,1,0:T(8,128)(2,1)S(1)}, bf16[1,256,256]{2,1,0:T(8,128)(2,1)S(1)}, u32[]{:S(2)}, u32[]{:S(2)}) collective-permute-start(bf16[1,256,256]{2,1,0:T(8,128)(2,1)S(1)} %collective-permute-done.2), channel_id=1, source_target_pairs={{32,0},{64,32},{96,64},{128,96},{160,128},{192,160},{224,192},{0,2... | collective-permute-start | bytes 393224 | tf_op jit(solution)/shard_map/cond/branch_0_fun/ppermute | solution.py:22
  16.5 13.2 %collective-permute-start.7 = (bf16[4,256,256]{2,1,0:T(8,128)(2,1)S(1)}, bf16[4,256,256]{2,1,0:T(8,128)(2,1)S(1)}, u32[]{:S(2)}, u32[]{:S(2)}) collective-permute-start(bf16[4,256,256]{2,1,0:T(8,128)(2,1)S(1)} %constant_dynamic-update-slice_fusion.refs_0_), channel_id=1, source_target_pairs={{8,0},{16,8},{24,16},{0,24},{9,1},{17,9},{25,17},{1,25},{10,2},{18... | collective-permute-start | bytes 1572872 | tf_op jit(solution)/shard_map/cond/branch_0_fun/ppermute | solution.py:26
  19.3 7.5 %collective-permute-start.6 = (bf16[1,256,256]{2,1,0:T(8,128)(2,1)S(1)}, bf16[1,256,256]{2,1,0:T(8,128)(2,1)S(1)}, u32[]{:S(2)}, u32[]{:S(2)}) collective-permute-start(bf16[1,256,256]{2,1,0:T(8,128)(2,1)S(1)} %collective-permute-done.2), channel_id=1, source_target_pairs={{64,0},{96,32},{128,64},{160,96},{192,128},{224,160},{0,192},{32,2... | collective-permute-start | bytes 393224 | tf_op jit(solution)/shard_map/cond/branch_0_fun/ppermute | solution.py:22
  19.4 6.8 %collective-permute-start.5 = (bf16[1,256,256]{2,1,0:T(8,128)(2,1)S(1)}, bf16[1,256,256]{2,1,0:T(8,128)(2,1)S(1)}, u32[]{:S(2)}, u32[]{:S(2)}) collective-permute-start(bf16[1,256,256]{2,1,0:T(8,128)(2,1)S(1)} %collective-permute-done.3), channel_id=1, source_target_pairs={{224,0},{0,32},{32,64},{64,96},{96,128},{128,160},{160,192},{192,2... | collective-permute-start | bytes 393224 | tf_op jit(solution)/shard_map/cond/branch_0_fun/ppermute | solution.py:22
  26.8 9.3 %collective-permute-start.10 = (bf16[4,256,256]{2,1,0:T(8,128)(2,1)S(1)}, bf16[4,256,256]{2,1,0:T(8,128)(2,1)S(1)}, u32[]{:S(2)}, u32[]{:S(2)}) collective-permute-start(bf16[4,256,256]{2,1,0:T(8,128)(2,1)S(1)} %constant_dynamic-update-slice_fusion.4.refs_1_), channel_id=1, source_target_pairs={{24,0},{0,8},{8,16},{16,24},{25,1},{1,9},{9,17},{17,25},{26,2},{2,... | collective-permute-start | bytes 1572872 | tf_op jit(solution)/shard_map/cond/branch_0_fun/ppermute | solution.py:26
  26.9 15.1 %collective-permute-start.8 = (bf16[4,256,256]{2,1,0:T(8,128)(2,1)S(1)}, bf16[4,256,256]{2,1,0:T(8,128)(2,1)S(1)}, u32[]{:S(2)}, u32[]{:S(2)}) collective-permute-start(bf16[4,256,256]{2,1,0:T(8,128)(2,1)S(1)} %constant_dynamic-update-slice_fusion.refs_0_), channel_id=1, source_target_pairs={{24,0},{0,8},{8,16},{16,24},{25,1},{1,9},{9,17},{17,25},{26,2},{2,... | collective-permute-start | bytes 1572872 | tf_op jit(solution)/shard_map/cond/branch_0_fun/ppermute | solution.py:26
  27.0 15.1 %collective-permute-start.9 = (bf16[4,256,256]{2,1,0:T(8,128)(2,1)S(1)}, bf16[4,256,256]{2,1,0:T(8,128)(2,1)S(1)}, u32[]{:S(2)}, u32[]{:S(2)}) collective-permute-start(bf16[4,256,256]{2,1,0:T(8,128)(2,1)S(1)} %constant_dynamic-update-slice_fusion.4.refs_1_), channel_id=1, source_target_pairs={{8,0},{16,8},{24,16},{0,24},{9,1},{17,9},{25,17},{1,25},{10,2},{18... | collective-permute-start | bytes 1572872 | tf_op jit(solution)/shard_map/cond/branch_0_fun/ppermute | solution.py:26
  29.7 12.4 %collective-permute-start.11 = (bf16[4,256,256]{2,1,0:T(8,128)(2,1)S(1)}, bf16[4,256,256]{2,1,0:T(8,128)(2,1)S(1)}, u32[]{:S(2)}, u32[]{:S(2)}) collective-permute-start(bf16[4,256,256]{2,1,0:T(8,128)(2,1)S(1)} %collective-permute-done.7.refs_2_), channel_id=1, source_target_pairs={{8,0},{16,8},{24,16},{0,24},{9,1},{17,9},{25,17},{1,25},{10,2},{18... | collective-permute-start | bytes 1572872 | tf_op jit(solution)/shard_map/cond/branch_0_fun/ppermute | solution.py:26
  36.1 11.5 %collective-permute-start.12 = (bf16[4,256,256]{2,1,0:T(8,128)(2,1)S(1)}, bf16[4,256,256]{2,1,0:T(8,128)(2,1)S(1)}, u32[]{:S(2)}, u32[]{:S(2)}) collective-permute-start(bf16[4,256,256]{2,1,0:T(8,128)(2,1)S(1)} %collective-permute-done.10.refs_5_), channel_id=1, source_target_pairs={{24,0},{0,8},{8,16},{16,24},{25,1},{1,9},{9,17},{17,25},{26,2},{2,... | collective-permute-start | bytes 1572872 | tf_op jit(solution)/shard_map/cond/branch_0_fun/ppermute | solution.py:26
where the time goes:
time: 109 us
  blocking collectives  43.3 us (40%)
  waiting for transfers between devices  25.7 us (24%)
  starting transfers between devices  19.8 us (18%)
  Pallas kernels  16.4 us (15%)
  local copies, waits for them, and re-layouts  3.46 us (3%)
    all_to_all x1, blocking collectives, shards(): lax.all_to_all(grouped, ('x', 'c'), split_axis=0, concat_axis=0, tiled=True)  22.7 us
    all_to_all x1, blocking collectives, run(): lax.all_to_all(by_target, ('z', 'y'), split_axis=0, concat_axis=0, tiled=...  20.5 us
    pallas_call x1, Pallas kernels, project(): pl.pallas_call(functools.partial(project_kernel, [m for _, m in pieces]),...  16.4 us
    ppermute x6, waiting for transfers between devices, from_y(): return lax.ppermute(value, 'y', [((s + step) % NY, s) for s in range(NY)])  15.9 us
    ppermute x7, starting transfers between devices, from_z(): return lax.ppermute(value, 'z', [((s + step) % NZ, s) for s in range(NZ)])  12.8 us
    ppermute x7, waiting for transfers between devices, from_z(): return lax.ppermute(value, 'z', [((s + step) % NZ, s) for s in range(NZ)])  9.79 us
    ppermute x6, starting transfers between devices, from_y(): return lax.ppermute(value, 'y', [((s + step) % NY, s) for s in range(NY)])  7.02 us
  transfers between devices with their start and end apart: 13, of which 7 were waited for; matrix products, arithmetic and copies ran while one was open for 2% of the time, Pallas kernels for 0%

commit v1 on v0

--- a/solution.py
+++ b/solution.py
@@ -148,6 +148,30 @@
     return lax.all_to_all(by_target, ("z", "y"), split_axis=0, concat_axis=0, tiled=True)
 
 
+def side_by_side_kernel(heads_ref, out_ref, sems):
+    heads, _, _, rows = heads_ref.shape
+    copies = [
+        pltpu.make_async_copy(heads_ref.at[t], out_ref.at[:, :, pl.ds(t * rows, rows)], sems.at[t]) for t in range(heads)
+    ]
+    for copy in copies:
+        copy.start()
+    for copy in copies:
+        copy.wait()
+
+
+def side_by_side(landed):
+    heads, slots, cap, rows = landed.shape
+    anywhere = pl.BlockSpec(memory_space=pl.ANY)
+    return pl.pallas_call(
+        side_by_side_kernel,
+        out_shape=jax.ShapeDtypeStruct((slots, cap, heads * rows), landed.dtype),
+        in_specs=[anywhere],
+        out_specs=anywhere,
+        scratch_shapes=[pltpu.SemaphoreType.DMA((heads,))],
+        name="side_by_side",
+    )(landed)
+
+
 def shards(hidden, norm_gain, kv_weight, lengths, owner):
     _, cap, width = hidden.shape
     rows, cols = kv_weight.shape
@@ -167,8 +191,7 @@
         own, hidden, norm_gain, place, owner, lengths, cosine, sine,
     )
     landed = lax.all_to_all(grouped, ("x", "c"), split_axis=0, concat_axis=0, tiled=True)
-    landed = landed.reshape(-1, NY, cap, rows)
-    return jnp.transpose(landed, (1, 2, 0, 3)).reshape(NY, cap, -1)
+    return side_by_side(landed.reshape(-1, NY, cap, rows))
 
 
 def solution(mesh):

time: 109 us -> 133 us (1.22)
  Pallas kernels: 16.4 us -> 41.4 us
  local copies, waits for them, and re-layouts: 3.46 us -> 1.78 us
    pallas_call x0 -> x1, Pallas kernels: none -> 25 us  [side_by_side(): pl.pallas_call(side_by_side_kernel, out_shape=jax.ShapeDtypeStruct((slots...]
    reshape x2 -> x0, local copies, waits for them, and re-layouts: 1.67 us -> none  [the longest x1 1.24 us: shards(): return jnp.transpose(landed, (1, 2, 0, 3)).reshape(NY, cap, -1)]
  transfers between devices with their start and end apart: 13 -> 13, of which waited for: 7 -> 7; matrix products, arithmetic and copies ran while one was open for 2% -> 1% of each run, Pallas kernels for 0% -> 0%
where the time goes in v1:
time: 133 us
  blocking collectives  43.4 us (33%)
  Pallas kernels  41.4 us (31%)
  waiting for transfers between devices  25.7 us (19%)
  starting transfers between devices  19.8 us (15%)
  local copies, waits for them, and re-layouts  1.78 us (1%)
    pallas_call x1, Pallas kernels, side_by_side(): pl.pallas_call(side_by_side_kernel, out_shape=jax.ShapeDtypeStruct((slots...  25 us
    all_to_all x1, blocking collectives, shards(): lax.all_to_all(grouped, ('x', 'c'), split_axis=0, concat_axis=0, tiled=True)  22.9 us
    all_to_all x1, blocking collectives, run(): lax.all_to_all(by_target, ('z', 'y'), split_axis=0, concat_axis=0, tiled=...  20.5 us
    pallas_call x1, Pallas kernels, project(): pl.pallas_call(functools.partial(project_kernel, [m for _, m in pieces]),...  16.4 us
    ppermute x6, waiting for transfers between devices, from_y(): return lax.ppermute(value, 'y', [((s + step) % NY, s) for s in range(NY)])  15.9 us
    ppermute x7, starting transfers between devices, from_z(): return lax.ppermute(value, 'z', [((s + step) % NZ, s) for s in range(NZ)])  12.8 us
    ppermute x7, waiting for transfers between devices, from_z(): return lax.ppermute(value, 'z', [((s + step) % NZ, s) for s in range(NZ)])  9.79 us
    ppermute x6, starting transfers between devices, from_y(): return lax.ppermute(value, 'y', [((s + step) % NY, s) for s in range(NY)])  7.02 us
  transfers between devices with their start and end apart: 13, of which 7 were waited for; matrix products, arithmetic and copies ran while one was open for 1% of the time, Pallas kernels for 0%

profile of v1, /device:TPU:1, one launch (start us, length us, event | category | flops | bytes accessed | tf_op | source)
XLA Modules:
  0.0 132.6 jit_solution(994799686431889948)
XLA Ops:
  0.0 0.1 fusion.2
  0.3 84.3 %conditional.1 = (bf16[32,48,256]{2,1,0:T(8,128)(2,1)S(1)}) conditional(s32[]{:T(128)} %convert_element_type.3, (bf16[8192]{0:T(1024)(128)(2,1)}, bf16[1,256,256]{2,1,0:T(8,128)(2,1)}, s32[2]{0:T(128)S(1)}, s32[32]{0:T(128)}, s32[32]{0:T(128)}, /*index=5*/bf16[32,48,8192]{2,1,0:T(8,128)(2,1)}, f32[48,128]{1,0:T(8,128)S(1)}, ...), branch_computations={%region_0.0_spmd, %region_1.0_spmd} | conditional | flops 6442450944 | bytes 45122064 | solution.py:187
  0.3 6.9 %collective-permute-start.2 = (bf16[1,256,256]{2,1,0:T(8,128)(2,1)}, bf16[1,256,256]{2,1,0:T(8,128)(2,1)S(1)}, u32[]{:S(2)}, u32[]{:S(2)}) collective-permute-start(bf16[1,256,256]{2,1,0:T(8,128)(2,1)} %get-tuple-element.47), channel_id=1, source_target_pairs={{64,0},{96,32},{128,64},{160,96},{192,128},{224,160},{0,192},{32,2... | collective-permute-start | bytes 393224 | tf_op jit(solution)/shard_map/cond/branch_0_fun/ppermute | solution.py:22
  7.2 0.7 collective-permute-start
  8.0 1.2 collective-permute-start.3
  9.2 1.0 constant_dynamic-update-slice_fusion.3
  10.1 0.8 collective-permute-done.2
  10.9 2.1 %collective-permute-start.4 = (bf16[1,256,256]{2,1,0:T(8,128)(2,1)S(1)}, bf16[1,256,256]{2,1,0:T(8,128)(2,1)S(1)}, u32[]{:S(2)}, u32[]{:S(2)}) collective-permute-start(bf16[1,256,256]{2,1,0:T(8,128)(2,1)S(1)} %collective-permute-done.2), channel_id=1, source_target_pairs={{32,0},{64,32},{96,64},{128,96},{160,128},{192,160},{224,192},{0,2... | collective-permute-start | bytes 393224 | tf_op jit(solution)/shard_map/cond/branch_0_fun/ppermute | solution.py:22
  13.0 3.4 %collective-permute-done.1 = bf16[1,256,256]{2,1,0:T(8,128)(2,1)S(1)} collective-permute-done((bf16[1,256,256]{2,1,0:T(8,128)(2,1)}, bf16[1,256,256]{2,1,0:T(8,128)(2,1)S(1)}, u32[]{:S(2)}, u32[]{:S(2)}) %collective-permute-start.1) | collective-permute-done | bytes 131104 | tf_op jit(solution)/shard_map/cond/branch_0_fun/ppermute | solution.py:22
  16.5 2.8 %collective-permute-start.7 = (bf16[4,256,256]{2,1,0:T(8,128)(2,1)S(1)}, bf16[4,256,256]{2,1,0:T(8,128)(2,1)S(1)}, u32[]{:S(2)}, u32[]{:S(2)}) collective-permute-start(bf16[4,256,256]{2,1,0:T(8,128)(2,1)S(1)} %constant_dynamic-update-slice_fusion.refs_0_), channel_id=1, source_target_pairs={{8,0},{16,8},{24,16},{0,24},{9,1},{17,9},{25,17},{1,25},{10,2},{18... | collective-permute-start | bytes 1572872 | tf_op jit(solution)/shard_map/cond/branch_0_fun/ppermute | solution.py:26
  19.4 1.8 %collective-permute-start.5 = (bf16[1,256,256]{2,1,0:T(8,128)(2,1)S(1)}, bf16[1,256,256]{2,1,0:T(8,128)(2,1)S(1)}, u32[]{:S(2)}, u32[]{:S(2)}) collective-permute-start(bf16[1,256,256]{2,1,0:T(8,128)(2,1)S(1)} %collective-permute-done.3), channel_id=1, source_target_pairs={{224,0},{0,32},{32,64},{64,96},{96,128},{128,160},{160,192},{192,2... | collective-permute-start | bytes 393224 | tf_op jit(solution)/shard_map/cond/branch_0_fun/ppermute | solution.py:22
  21.2 4.9 %collective-permute-done.5 = bf16[1,256,256]{2,1,0:T(8,128)(2,1)S(1)} collective-permute-done((bf16[1,256,256]{2,1,0:T(8,128)(2,1)S(1)}, bf16[1,256,256]{2,1,0:T(8,128)(2,1)S(1)}, u32[]{:S(2)}, u32[]{:S(2)}) %collective-permute-start.5) | collective-permute-done | bytes 131104 | tf_op jit(solution)/shard_map/cond/branch_0_fun/ppermute | solution.py:22
  26.2 0.7 collective-permute-done.6
  26.8 0.1 collective-permute-start.10
  27.0 2.7 %collective-permute-start.9 = (bf16[4,256,256]{2,1,0:T(8,128)(2,1)S(1)}, bf16[4,256,256]{2,1,0:T(8,128)(2,1)S(1)}, u32[]{:S(2)}, u32[]{:S(2)}) collective-permute-start(bf16[4,256,256]{2,1,0:T(8,128)(2,1)S(1)} %constant_dynamic-update-slice_fusion.4.refs_1_), channel_id=1, source_target_pairs={{8,0},{16,8},{24,16},{0,24},{9,1},{17,9},{25,17},{1,25},{10,2},{18... | collective-permute-start | bytes 1572872 | tf_op jit(solution)/shard_map/cond/branch_0_fun/ppermute | solution.py:26
  29.7 1.4 %collective-permute-start.11 = (bf16[4,256,256]{2,1,0:T(8,128)(2,1)S(1)}, bf16[4,256,256]{2,1,0:T(8,128)(2,1)S(1)}, u32[]{:S(2)}, u32[]{:S(2)}) collective-permute-start(bf16[4,256,256]{2,1,0:T(8,128)(2,1)S(1)} %collective-permute-done.7.refs_2_), channel_id=1, source_target_pairs={{8,0},{16,8},{24,16},{0,24},{9,1},{17,9},{25,17},{1,25},{10,2},{18... | collective-permute-start | bytes 1572872 | tf_op jit(solution)/shard_map/cond/branch_0_fun/ppermute | solution.py:26
  31.1 5.1 %collective-permute-done.10.refs_5_ = bf16[4,256,256]{2,1,0:T(8,128)(2,1)S(1)} collective-permute-done((bf16[4,256,256]{2,1,0:T(8,128)(2,1)S(1)}, bf16[4,256,256]{2,1,0:T(8,128)(2,1)S(1)}, u32[]{:S(2)}, u32[]{:S(2)}) %collective-permute-start.10) | collective-permute-done | bytes 524320 | tf_op jit(solution)/shard_map/cond/branch_0_fun/ppermute | solution.py:26
  36.2 0.7 reshape.15.gain_ref
  36.9 5.2 %collective-permute-done.8.refs_3_ = bf16[4,256,256]{2,1,0:T(8,128)(2,1)S(1)} collective-permute-done((bf16[4,256,256]{2,1,0:T(8,128)(2,1)S(1)}, bf16[4,256,256]{2,1,0:T(8,128)(2,1)S(1)}, u32[]{:S(2)}, u32[]{:S(2)}) %collective-permute-start.8) | collective-permute-done | bytes 524320 | tf_op jit(solution)/shard_map/cond/branch_0_fun/ppermute | solution.py:26
  42.1 5.6 %collective-permute-done.12.refs_7_ = bf16[4,256,256]{2,1,0:T(8,128)(2,1)S(1)} collective-permute-done((bf16[4,256,256]{2,1,0:T(8,128)(2,1)S(1)}, bf16[4,256,256]{2,1,0:T(8,128)(2,1)S(1)}, u32[]{:S(2)}, u32[]{:S(2)}) %collective-permute-start.12) | collective-permute-done | bytes 524320 | tf_op jit(solution)/shard_map/cond/branch_0_fun/ppermute | solution.py:26
  47.7 16.4 %project.2 = bf16[32,48,256]{2,1,0:T(8,128)(2,1)S(1)} custom-call(s32[2]{0:T(128)S(1)} %get-tuple-element.40.place_ref, s32[32]{0:T(128)} %get-tuple-element.41.slot_ref, s32[32]{0:T(128)} %get-tuple-element.42.length_ref, bf16[32,48,8192]{2,1,0:T(8,128)(2,1)} %get-tuple-element.43.hidden_ref, f32[48,128]{1,0:T(8,128)S(1)} %get-tuple-element.44.cosine_ref, ...), custom_call_target="tpu_custom_call" | custom-call | flops 6442450944 | bytes 25165824 | tf_op jit(solution)/shard_map/cond/branch_0_fun/project/pallas_call | solution.py:128
  64.1 20.5 %all_to_all.13 = bf16[32,48,256]{2,1,0:T(8,128)(2,1)S(1)} all-to-all(bf16[32,48,256]{2,1,0:T(8,128)(2,1)S(1)} %project.2), channel_id=1, replica_groups=mesh['z'=8,'y'=4,'x'=4,'c'=2] {'z','y'}, dimensions={0} | all-to-all | bytes 1572864 | tf_op jit(solution)/shard_map/cond/branch_0_fun/all_to_all | solution.py:148
  84.6 22.9 %all_to_all.15 = bf16[32,48,256]{2,1,0:T(8,128)(2,1)} all-to-all(bf16[32,48,256]{2,1,0:T(8,128)(2,1)S(1)} %get-tuple-element.61), channel_id=1, replica_groups=mesh['z'=8,'y'=4,'x'=4,'c'=2] {'x','c'}, dimensions={0} | all-to-all | bytes 1572864 | tf_op jit(solution)/shard_map/all_to_all | solution.py:193
  107.4 25.0 %side_by_side.1 = bf16[4,48,2048]{2,1,0:T(8,128)(2,1)} custom-call(bf16[8,4,48,256]{3,2,1,0:T(8,128)(2,1)} %bitcast.4), custom_call_target="tpu_custom_call" | custom-call | tf_op jit(solution)/shard_map/side_by_side/pallas_call | solution.py:165
  (20 shorter events, 0.4 us)
Async XLA Ops:
  0.3 10.6 %collective-permute-start.2 = (bf16[1,256,256]{2,1,0:T(8,128)(2,1)}, bf16[1,256,256]{2,1,0:T(8,128)(2,1)S(1)}, u32[]{:S(2)}, u32[]{:S(2)}) collective-permute-start(bf16[1,256,256]{2,1,0:T(8,128)(2,1)} %get-tuple-element.47), channel_id=1, source_target_pairs={{64,0},{96,32},{128,64},{160,96},{192,128},{224,160},{0,192},{32,2... | collective-permute-start | bytes 393224 | tf_op jit(solution)/shard_map/cond/branch_0_fun/ppermute | solution.py:22
  7.2 5.8 %collective-permute-start = (bf16[1,256,256]{2,1,0:T(8,128)(2,1)}, bf16[1,256,256]{2,1,0:T(8,128)(2,1)S(1)}, u32[]{:S(2)}, u32[]{:S(2)}) collective-permute-start(bf16[1,256,256]{2,1,0:T(8,128)(2,1)} %get-tuple-element.47), channel_id=1, source_target_pairs={{32,0},{64,32},{96,64},{128,96},{160,128},{192,160},{224,192},{0,2... | collective-permute-start | bytes 393224 | tf_op jit(solution)/shard_map/cond/branch_0_fun/ppermute | solution.py:22
  8.0 11.4 %collective-permute-start.3 = (bf16[1,256,256]{2,1,0:T(8,128)(2,1)}, bf16[1,256,256]{2,1,0:T(8,128)(2,1)S(1)}, u32[]{:S(2)}, u32[]{:S(2)}) collective-permute-start(bf16[1,256,256]{2,1,0:T(8,128)(2,1)} %get-tuple-element.47), channel_id=1, source_target_pairs={{192,0},{224,32},{0,64},{32,96},{64,128},{96,160},{128,192},{160,2... | collective-permute-start | bytes 393224 | tf_op jit(solution)/shard_map/cond/branch_0_fun/ppermute | solution.py:22
  9.2 7.3 %collective-permute-start.1 = (bf16[1,256,256]{2,1,0:T(8,128)(2,1)}, bf16[1,256,256]{2,1,0:T(8,128)(2,1)S(1)}, u32[]{:S(2)}, u32[]{:S(2)}) collective-permute-start(bf16[1,256,256]{2,1,0:T(8,128)(2,1)} %get-tuple-element.47), channel_id=1, source_target_pairs={{224,0},{0,32},{32,64},{64,96},{96,128},{128,160},{160,192},{192,2... | collective-permute-start | bytes 393224 | tf_op jit(solution)/shard_map/cond/branch_0_fun/ppermute | solution.py:22
  10.9 10.3 %collective-permute-start.4 = (bf16[1,256,256]{2,1,0:T(8,128)(2,1)S(1)}, bf16[1,256,256]{2,1,0:T(8,128)(2,1)S(1)}, u32[]{:S(2)}, u32[]{:S(2)}) collective-permute-start(bf16[1,256,256]{2,1,0:T(8,128)(2,1)S(1)} %collective-permute-done.2), channel_id=1, source_target_pairs={{32,0},{64,32},{96,64},{128,96},{160,128},{192,160},{224,192},{0,2... | collective-permute-start | bytes 393224 | tf_op jit(solution)/shard_map/cond/branch_0_fun/ppermute | solution.py:22
  16.5 13.2 %collective-permute-start.7 = (bf16[4,256,256]{2,1,0:T(8,128)(2,1)S(1)}, bf16[4,256,256]{2,1,0:T(8,128)(2,1)S(1)}, u32[]{:S(2)}, u32[]{:S(2)}) collective-permute-start(bf16[4,256,256]{2,1,0:T(8,128)(2,1)S(1)} %constant_dynamic-update-slice_fusion.refs_0_), channel_id=1, source_target_pairs={{8,0},{16,8},{24,16},{0,24},{9,1},{17,9},{25,17},{1,25},{10,2},{18... | collective-permute-start | bytes 1572872 | tf_op jit(solution)/shard_map/cond/branch_0_fun/ppermute | solution.py:26
  19.3 7.5 %collective-permute-start.6 = (bf16[1,256,256]{2,1,0:T(8,128)(2,1)S(1)}, bf16[1,256,256]{2,1,0:T(8,128)(2,1)S(1)}, u32[]{:S(2)}, u32[]{:S(2)}) collective-permute-start(bf16[1,256,256]{2,1,0:T(8,128)(2,1)S(1)} %collective-permute-done.2), channel_id=1, source_target_pairs={{64,0},{96,32},{128,64},{160,96},{192,128},{224,160},{0,192},{32,2... | collective-permute-start | bytes 393224 | tf_op jit(solution)/shard_map/cond/branch_0_fun/ppermute | solution.py:22
  19.4 6.8 %collective-permute-start.5 = (bf16[1,256,256]{2,1,0:T(8,128)(2,1)S(1)}, bf16[1,256,256]{2,1,0:T(8,128)(2,1)S(1)}, u32[]{:S(2)}, u32[]{:S(2)}) collective-permute-start(bf16[1,256,256]{2,1,0:T(8,128)(2,1)S(1)} %collective-permute-done.3), channel_id=1, source_target_pairs={{224,0},{0,32},{32,64},{64,96},{96,128},{128,160},{160,192},{192,2... | collective-permute-start | bytes 393224 | tf_op jit(solution)/shard_map/cond/branch_0_fun/ppermute | solution.py:22
  26.8 9.3 %collective-permute-start.10 = (bf16[4,256,256]{2,1,0:T(8,128)(2,1)S(1)}, bf16[4,256,256]{2,1,0:T(8,128)(2,1)S(1)}, u32[]{:S(2)}, u32[]{:S(2)}) collective-permute-start(bf16[4,256,256]{2,1,0:T(8,128)(2,1)S(1)} %constant_dynamic-update-slice_fusion.4.refs_1_), channel_id=1, source_target_pairs={{24,0},{0,8},{8,16},{16,24},{25,1},{1,9},{9,17},{17,25},{26,2},{2,... | collective-permute-start | bytes 1572872 | tf_op jit(solution)/shard_map/cond/branch_0_fun/ppermute | solution.py:26
  26.9 15.1 %collective-permute-start.8 = (bf16[4,256,256]{2,1,0:T(8,128)(2,1)S(1)}, bf16[4,256,256]{2,1,0:T(8,128)(2,1)S(1)}, u32[]{:S(2)}, u32[]{:S(2)}) collective-permute-start(bf16[4,256,256]{2,1,0:T(8,128)(2,1)S(1)} %constant_dynamic-update-slice_fusion.refs_0_), channel_id=1, source_target_pairs={{24,0},{0,8},{8,16},{16,24},{25,1},{1,9},{9,17},{17,25},{26,2},{2,... | collective-permute-start | bytes 1572872 | tf_op jit(solution)/shard_map/cond/branch_0_fun/ppermute | solution.py:26
  27.0 15.1 %collective-permute-start.9 = (bf16[4,256,256]{2,1,0:T(8,128)(2,1)S(1)}, bf16[4,256,256]{2,1,0:T(8,128)(2,1)S(1)}, u32[]{:S(2)}, u32[]{:S(2)}) collective-permute-start(bf16[4,256,256]{2,1,0:T(8,128)(2,1)S(1)} %constant_dynamic-update-slice_fusion.4.refs_1_), channel_id=1, source_target_pairs={{8,0},{16,8},{24,16},{0,24},{9,1},{17,9},{25,17},{1,25},{10,2},{18... | collective-permute-start | bytes 1572872 | tf_op jit(solution)/shard_map/cond/branch_0_fun/ppermute | solution.py:26
  29.7 12.4 %collective-permute-start.11 = (bf16[4,256,256]{2,1,0:T(8,128)(2,1)S(1)}, bf16[4,256,256]{2,1,0:T(8,128)(2,1)S(1)}, u32[]{:S(2)}, u32[]{:S(2)}) collective-permute-start(bf16[4,256,256]{2,1,0:T(8,128)(2,1)S(1)} %collective-permute-done.7.refs_2_), channel_id=1, source_target_pairs={{8,0},{16,8},{24,16},{0,24},{9,1},{17,9},{25,17},{1,25},{10,2},{18... | collective-permute-start | bytes 1572872 | tf_op jit(solution)/shard_map/cond/branch_0_fun/ppermute | solution.py:26
  36.1 11.5 %collective-permute-start.12 = (bf16[4,256,256]{2,1,0:T(8,128)(2,1)S(1)}, bf16[4,256,256]{2,1,0:T(8,128)(2,1)S(1)}, u32[]{:S(2)}, u32[]{:S(2)}) collective-permute-start(bf16[4,256,256]{2,1,0:T(8,128)(2,1)S(1)} %collective-permute-done.10.refs_5_), channel_id=1, source_target_pairs={{24,0},{0,8},{8,16},{16,24},{25,1},{1,9},{9,17},{17,25},{26,2},{2,... | collective-permute-start | bytes 1572872 | tf_op jit(solution)/shard_map/cond/branch_0_fun/ppermute | solution.py:26

commit v2 on v0

--- a/solution.py
+++ b/solution.py
@@ -148,6 +148,25 @@
     return lax.all_to_all(by_target, ("z", "y"), split_axis=0, concat_axis=0, tiled=True)
 
 
+def side_by_side_kernel(heads_ref, out_ref):
+    heads, _, _, rows = heads_ref.shape
+    for t in range(heads):
+        out_ref[:, :, t * rows : (t + 1) * rows] = heads_ref[t]
+
+
+def side_by_side(landed):
+    heads, slots, cap, rows = landed.shape
+    vmem = pl.BlockSpec(memory_space=pltpu.VMEM)
+    return pl.pallas_call(
+        side_by_side_kernel,
+        out_shape=jax.ShapeDtypeStruct((slots, cap, heads * rows), landed.dtype),
+        in_specs=[vmem],
+        out_specs=vmem,
+        compiler_params=pltpu.CompilerParams(vmem_limit_bytes=VMEM_LIMIT),
+        name="side_by_side",
+    )(landed)
+
+
 def shards(hidden, norm_gain, kv_weight, lengths, owner):
     _, cap, width = hidden.shape
     rows, cols = kv_weight.shape
@@ -167,8 +186,7 @@
         own, hidden, norm_gain, place, owner, lengths, cosine, sine,
     )
     landed = lax.all_to_all(grouped, ("x", "c"), split_axis=0, concat_axis=0, tiled=True)
-    landed = landed.reshape(-1, NY, cap, rows)
-    return jnp.transpose(landed, (1, 2, 0, 3)).reshape(NY, cap, -1)
+    return side_by_side(landed.reshape(-1, NY, cap, rows))
 
 
 def solution(mesh):

time: 109 us -> 109 us (level)
  local copies, waits for them, and re-layouts: 3.46 us -> 1.78 us
    reshape x2 -> x0, local copies, waits for them, and re-layouts: 1.67 us -> none  [the longest x1 1.24 us: shards(): return jnp.transpose(landed, (1, 2, 0, 3)).reshape(NY, cap, -1)]
where the time goes in v2:
time: 109 us; the launch traced here: 108 us
  blocking collectives  43.3 us (40%)
  waiting for transfers between devices  25.7 us (24%)
  starting transfers between devices  19.8 us (18%)
  Pallas kernels  17.3 us (16%)
  local copies, waits for them, and re-layouts  1.78 us (2%)
    all_to_all x1, blocking collectives, shards(): lax.all_to_all(grouped, ('x', 'c'), split_axis=0, concat_axis=0, tiled=True)  22.7 us
    all_to_all x1, blocking collectives, run(): lax.all_to_all(by_target, ('z', 'y'), split_axis=0, concat_axis=0, tiled=...  20.5 us
    pallas_call x1, Pallas kernels, project(): pl.pallas_call(functools.partial(project_kernel, [m for _, m in pieces]),...  16.4 us
    ppermute x6, waiting for transfers between devices, from_y(): return lax.ppermute(value, 'y', [((s + step) % NY, s) for s in range(NY)])  15.9 us
    ppermute x7, starting transfers between devices, from_z(): return lax.ppermute(value, 'z', [((s + step) % NZ, s) for s in range(NZ)])  12.8 us
    ppermute x7, waiting for transfers between devices, from_z(): return lax.ppermute(value, 'z', [((s + step) % NZ, s) for s in range(NZ)])  9.79 us
    ppermute x6, starting transfers between devices, from_y(): return lax.ppermute(value, 'y', [((s + step) % NY, s) for s in range(NY)])  7.02 us
  transfers between devices with their start and end apart: 13, of which 7 were waited for; matrix products, arithmetic and copies ran while one was open for 2% of the time, Pallas kernels for 0%

profile of v2, /device:TPU:1, one launch (start us, length us, event | category | flops | bytes accessed | tf_op | source)
XLA Modules:
  0.0 108.3 jit_solution(13117578655339956067)
XLA Ops:
  0.0 0.1 fusion.2
  0.3 84.3 %conditional.1 = (bf16[32,48,256]{2,1,0:T(8,128)(2,1)S(1)}) conditional(s32[]{:T(128)} %convert_element_type.3, (bf16[8192]{0:T(1024)(128)(2,1)}, bf16[1,256,256]{2,1,0:T(8,128)(2,1)}, s32[2]{0:T(128)S(1)}, s32[32]{0:T(128)}, s32[32]{0:T(128)}, /*index=5*/bf16[32,48,8192]{2,1,0:T(8,128)(2,1)}, f32[48,128]{1,0:T(8,128)S(1)}, ...), branch_computations={%region_0.0_spmd, %region_1.0_spmd} | conditional | flops 6442450944 | bytes 45122064 | solution.py:182
  0.3 6.9 %collective-permute-start.2 = (bf16[1,256,256]{2,1,0:T(8,128)(2,1)}, bf16[1,256,256]{2,1,0:T(8,128)(2,1)S(1)}, u32[]{:S(2)}, u32[]{:S(2)}) collective-permute-start(bf16[1,256,256]{2,1,0:T(8,128)(2,1)} %get-tuple-element.47), channel_id=1, source_target_pairs={{64,0},{96,32},{128,64},{160,96},{192,128},{224,160},{0,192},{32,2... | collective-permute-start | bytes 393224 | tf_op jit(solution)/shard_map/cond/branch_0_fun/ppermute | solution.py:22
  7.2 0.7 collective-permute-start
  8.0 1.2 %collective-permute-start.3 = (bf16[1,256,256]{2,1,0:T(8,128)(2,1)}, bf16[1,256,256]{2,1,0:T(8,128)(2,1)S(1)}, u32[]{:S(2)}, u32[]{:S(2)}) collective-permute-start(bf16[1,256,256]{2,1,0:T(8,128)(2,1)} %get-tuple-element.47), channel_id=1, source_target_pairs={{192,0},{224,32},{0,64},{32,96},{64,128},{96,160},{128,192},{160,2... | collective-permute-start | bytes 393224 | tf_op jit(solution)/shard_map/cond/branch_0_fun/ppermute | solution.py:22
  9.2 1.0 constant_dynamic-update-slice_fusion.3
  10.1 0.8 collective-permute-done.2
  10.9 2.1 %collective-permute-start.4 = (bf16[1,256,256]{2,1,0:T(8,128)(2,1)S(1)}, bf16[1,256,256]{2,1,0:T(8,128)(2,1)S(1)}, u32[]{:S(2)}, u32[]{:S(2)}) collective-permute-start(bf16[1,256,256]{2,1,0:T(8,128)(2,1)S(1)} %collective-permute-done.2), channel_id=1, source_target_pairs={{32,0},{64,32},{96,64},{128,96},{160,128},{192,160},{224,192},{0,2... | collective-permute-start | bytes 393224 | tf_op jit(solution)/shard_map/cond/branch_0_fun/ppermute | solution.py:22
  13.0 3.4 %collective-permute-done.1 = bf16[1,256,256]{2,1,0:T(8,128)(2,1)S(1)} collective-permute-done((bf16[1,256,256]{2,1,0:T(8,128)(2,1)}, bf16[1,256,256]{2,1,0:T(8,128)(2,1)S(1)}, u32[]{:S(2)}, u32[]{:S(2)}) %collective-permute-start.1) | collective-permute-done | bytes 131104 | tf_op jit(solution)/shard_map/cond/branch_0_fun/ppermute | solution.py:22
  16.5 2.8 %collective-permute-start.7 = (bf16[4,256,256]{2,1,0:T(8,128)(2,1)S(1)}, bf16[4,256,256]{2,1,0:T(8,128)(2,1)S(1)}, u32[]{:S(2)}, u32[]{:S(2)}) collective-permute-start(bf16[4,256,256]{2,1,0:T(8,128)(2,1)S(1)} %constant_dynamic-update-slice_fusion.refs_0_), channel_id=1, source_target_pairs={{8,0},{16,8},{24,16},{0,24},{9,1},{17,9},{25,17},{1,25},{10,2},{18... | collective-permute-start | bytes 1572872 | tf_op jit(solution)/shard_map/cond/branch_0_fun/ppermute | solution.py:26
  19.4 1.8 %collective-permute-start.5 = (bf16[1,256,256]{2,1,0:T(8,128)(2,1)S(1)}, bf16[1,256,256]{2,1,0:T(8,128)(2,1)S(1)}, u32[]{:S(2)}, u32[]{:S(2)}) collective-permute-start(bf16[1,256,256]{2,1,0:T(8,128)(2,1)S(1)} %collective-permute-done.3), channel_id=1, source_target_pairs={{224,0},{0,32},{32,64},{64,96},{96,128},{128,160},{160,192},{192,2... | collective-permute-start | bytes 393224 | tf_op jit(solution)/shard_map/cond/branch_0_fun/ppermute | solution.py:22
  21.2 4.9 %collective-permute-done.5 = bf16[1,256,256]{2,1,0:T(8,128)(2,1)S(1)} collective-permute-done((bf16[1,256,256]{2,1,0:T(8,128)(2,1)S(1)}, bf16[1,256,256]{2,1,0:T(8,128)(2,1)S(1)}, u32[]{:S(2)}, u32[]{:S(2)}) %collective-permute-start.5) | collective-permute-done | bytes 131104 | tf_op jit(solution)/shard_map/cond/branch_0_fun/ppermute | solution.py:22
  26.2 0.7 collective-permute-done.6
  26.8 0.1 collective-permute-start.10
  27.0 2.7 %collective-permute-start.9 = (bf16[4,256,256]{2,1,0:T(8,128)(2,1)S(1)}, bf16[4,256,256]{2,1,0:T(8,128)(2,1)S(1)}, u32[]{:S(2)}, u32[]{:S(2)}) collective-permute-start(bf16[4,256,256]{2,1,0:T(8,128)(2,1)S(1)} %constant_dynamic-update-slice_fusion.4.refs_1_), channel_id=1, source_target_pairs={{8,0},{16,8},{24,16},{0,24},{9,1},{17,9},{25,17},{1,25},{10,2},{18... | collective-permute-start | bytes 1572872 | tf_op jit(solution)/shard_map/cond/branch_0_fun/ppermute | solution.py:26
  29.7 1.4 %collective-permute-start.11 = (bf16[4,256,256]{2,1,0:T(8,128)(2,1)S(1)}, bf16[4,256,256]{2,1,0:T(8,128)(2,1)S(1)}, u32[]{:S(2)}, u32[]{:S(2)}) collective-permute-start(bf16[4,256,256]{2,1,0:T(8,128)(2,1)S(1)} %collective-permute-done.7.refs_2_), channel_id=1, source_target_pairs={{8,0},{16,8},{24,16},{0,24},{9,1},{17,9},{25,17},{1,25},{10,2},{18... | collective-permute-start | bytes 1572872 | tf_op jit(solution)/shard_map/cond/branch_0_fun/ppermute | solution.py:26
  31.1 5.1 %collective-permute-done.10.refs_5_ = bf16[4,256,256]{2,1,0:T(8,128)(2,1)S(1)} collective-permute-done((bf16[4,256,256]{2,1,0:T(8,128)(2,1)S(1)}, bf16[4,256,256]{2,1,0:T(8,128)(2,1)S(1)}, u32[]{:S(2)}, u32[]{:S(2)}) %collective-permute-start.10) | collective-permute-done | bytes 524320 | tf_op jit(solution)/shard_map/cond/branch_0_fun/ppermute | solution.py:26
  36.2 0.7 reshape.15.gain_ref
  36.9 5.2 %collective-permute-done.8.refs_3_ = bf16[4,256,256]{2,1,0:T(8,128)(2,1)S(1)} collective-permute-done((bf16[4,256,256]{2,1,0:T(8,128)(2,1)S(1)}, bf16[4,256,256]{2,1,0:T(8,128)(2,1)S(1)}, u32[]{:S(2)}, u32[]{:S(2)}) %collective-permute-start.8) | collective-permute-done | bytes 524320 | tf_op jit(solution)/shard_map/cond/branch_0_fun/ppermute | solution.py:26
  42.1 5.6 %collective-permute-done.12.refs_7_ = bf16[4,256,256]{2,1,0:T(8,128)(2,1)S(1)} collective-permute-done((bf16[4,256,256]{2,1,0:T(8,128)(2,1)S(1)}, bf16[4,256,256]{2,1,0:T(8,128)(2,1)S(1)}, u32[]{:S(2)}, u32[]{:S(2)}) %collective-permute-start.12) | collective-permute-done | bytes 524320 | tf_op jit(solution)/shard_map/cond/branch_0_fun/ppermute | solution.py:26
  47.7 16.4 %project.2 = bf16[32,48,256]{2,1,0:T(8,128)(2,1)S(1)} custom-call(s32[2]{0:T(128)S(1)} %get-tuple-element.40.place_ref, s32[32]{0:T(128)} %get-tuple-element.41.slot_ref, s32[32]{0:T(128)} %get-tuple-element.42.length_ref, bf16[32,48,8192]{2,1,0:T(8,128)(2,1)} %get-tuple-element.43.hidden_ref, f32[48,128]{1,0:T(8,128)S(1)} %get-tuple-element.44.cosine_ref, ...), custom_call_target="tpu_custom_call" | custom-call | flops 6442450944 | bytes 25165824 | tf_op jit(solution)/shard_map/cond/branch_0_fun/project/pallas_call | solution.py:128
  64.1 20.5 %all_to_all.13 = bf16[32,48,256]{2,1,0:T(8,128)(2,1)S(1)} all-to-all(bf16[32,48,256]{2,1,0:T(8,128)(2,1)S(1)} %project.2), channel_id=1, replica_groups=mesh['z'=8,'y'=4,'x'=4,'c'=2] {'z','y'}, dimensions={0} | all-to-all | bytes 1572864 | tf_op jit(solution)/shard_map/cond/branch_0_fun/all_to_all | solution.py:148
  84.6 22.7 %all_to_all.15 = bf16[32,48,256]{2,1,0:T(8,128)(2,1)S(1)} all-to-all(bf16[32,48,256]{2,1,0:T(8,128)(2,1)S(1)} %get-tuple-element.61), channel_id=1, replica_groups=mesh['z'=8,'y'=4,'x'=4,'c'=2] {'x','c'}, dimensions={0} | all-to-all | bytes 1572864 | tf_op jit(solution)/shard_map/all_to_all | solution.py:188
  107.3 1.0 side_by_side.1
  (20 shorter events, 0.4 us)
Async XLA Ops:
  0.3 10.6 %collective-permute-start.2 = (bf16[1,256,256]{2,1,0:T(8,128)(2,1)}, bf16[1,256,256]{2,1,0:T(8,128)(2,1)S(1)}, u32[]{:S(2)}, u32[]{:S(2)}) collective-permute-start(bf16[1,256,256]{2,1,0:T(8,128)(2,1)} %get-tuple-element.47), channel_id=1, source_target_pairs={{64,0},{96,32},{128,64},{160,96},{192,128},{224,160},{0,192},{32,2... | collective-permute-start | bytes 393224 | tf_op jit(solution)/shard_map/cond/branch_0_fun/ppermute | solution.py:22
  7.2 5.8 %collective-permute-start = (bf16[1,256,256]{2,1,0:T(8,128)(2,1)}, bf16[1,256,256]{2,1,0:T(8,128)(2,1)S(1)}, u32[]{:S(2)}, u32[]{:S(2)}) collective-permute-start(bf16[1,256,256]{2,1,0:T(8,128)(2,1)} %get-tuple-element.47), channel_id=1, source_target_pairs={{32,0},{64,32},{96,64},{128,96},{160,128},{192,160},{224,192},{0,2... | collective-permute-start | bytes 393224 | tf_op jit(solution)/shard_map/cond/branch_0_fun/ppermute | solution.py:22
  8.0 11.4 %collective-permute-start.3 = (bf16[1,256,256]{2,1,0:T(8,128)(2,1)}, bf16[1,256,256]{2,1,0:T(8,128)(2,1)S(1)}, u32[]{:S(2)}, u32[]{:S(2)}) collective-permute-start(bf16[1,256,256]{2,1,0:T(8,128)(2,1)} %get-tuple-element.47), channel_id=1, source_target_pairs={{192,0},{224,32},{0,64},{32,96},{64,128},{96,160},{128,192},{160,2... | collective-permute-start | bytes 393224 | tf_op jit(solution)/shard_map/cond/branch_0_fun/ppermute | solution.py:22
  9.2 7.3 %collective-permute-start.1 = (bf16[1,256,256]{2,1,0:T(8,128)(2,1)}, bf16[1,256,256]{2,1,0:T(8,128)(2,1)S(1)}, u32[]{:S(2)}, u32[]{:S(2)}) collective-permute-start(bf16[1,256,256]{2,1,0:T(8,128)(2,1)} %get-tuple-element.47), channel_id=1, source_target_pairs={{224,0},{0,32},{32,64},{64,96},{96,128},{128,160},{160,192},{192,2... | collective-permute-start | bytes 393224 | tf_op jit(solution)/shard_map/cond/branch_0_fun/ppermute | solution.py:22
  10.9 10.3 %collective-permute-start.4 = (bf16[1,256,256]{2,1,0:T(8,128)(2,1)S(1)}, bf16[1,256,256]{2,1,0:T(8,128)(2,1)S(1)}, u32[]{:S(2)}, u32[]{:S(2)}) collective-permute-start(bf16[1,256,256]{2,1,0:T(8,128)(2,1)S(1)} %collective-permute-done.2), channel_id=1, source_target_pairs={{32,0},{64,32},{96,64},{128,96},{160,128},{192,160},{224,192},{0,2... | collective-permute-start | bytes 393224 | tf_op jit(solution)/shard_map/cond/branch_0_fun/ppermute | solution.py:22
  16.5 13.2 %collective-permute-start.7 = (bf16[4,256,256]{2,1,0:T(8,128)(2,1)S(1)}, bf16[4,256,256]{2,1,0:T(8,128)(2,1)S(1)}, u32[]{:S(2)}, u32[]{:S(2)}) collective-permute-start(bf16[4,256,256]{2,1,0:T(8,128)(2,1)S(1)} %constant_dynamic-update-slice_fusion.refs_0_), channel_id=1, source_target_pairs={{8,0},{16,8},{24,16},{0,24},{9,1},{17,9},{25,17},{1,25},{10,2},{18... | collective-permute-start | bytes 1572872 | tf_op jit(solution)/shard_map/cond/branch_0_fun/ppermute | solution.py:26
  19.3 7.5 %collective-permute-start.6 = (bf16[1,256,256]{2,1,0:T(8,128)(2,1)S(1)}, bf16[1,256,256]{2,1,0:T(8,128)(2,1)S(1)}, u32[]{:S(2)}, u32[]{:S(2)}) collective-permute-start(bf16[1,256,256]{2,1,0:T(8,128)(2,1)S(1)} %collective-permute-done.2), channel_id=1, source_target_pairs={{64,0},{96,32},{128,64},{160,96},{192,128},{224,160},{0,192},{32,2... | collective-permute-start | bytes 393224 | tf_op jit(solution)/shard_map/cond/branch_0_fun/ppermute | solution.py:22
  19.4 6.8 %collective-permute-start.5 = (bf16[1,256,256]{2,1,0:T(8,128)(2,1)S(1)}, bf16[1,256,256]{2,1,0:T(8,128)(2,1)S(1)}, u32[]{:S(2)}, u32[]{:S(2)}) collective-permute-start(bf16[1,256,256]{2,1,0:T(8,128)(2,1)S(1)} %collective-permute-done.3), channel_id=1, source_target_pairs={{224,0},{0,32},{32,64},{64,96},{96,128},{128,160},{160,192},{192,2... | collective-permute-start | bytes 393224 | tf_op jit(solution)/shard_map/cond/branch_0_fun/ppermute | solution.py:22
  26.8 9.3 %collective-permute-start.10 = (bf16[4,256,256]{2,1,0:T(8,128)(2,1)S(1)}, bf16[4,256,256]{2,1,0:T(8,128)(2,1)S(1)}, u32[]{:S(2)}, u32[]{:S(2)}) collective-permute-start(bf16[4,256,256]{2,1,0:T(8,128)(2,1)S(1)} %constant_dynamic-update-slice_fusion.4.refs_1_), channel_id=1, source_target_pairs={{24,0},{0,8},{8,16},{16,24},{25,1},{1,9},{9,17},{17,25},{26,2},{2,... | collective-permute-start | bytes 1572872 | tf_op jit(solution)/shard_map/cond/branch_0_fun/ppermute | solution.py:26
  26.9 15.1 %collective-permute-start.8 = (bf16[4,256,256]{2,1,0:T(8,128)(2,1)S(1)}, bf16[4,256,256]{2,1,0:T(8,128)(2,1)S(1)}, u32[]{:S(2)}, u32[]{:S(2)}) collective-permute-start(bf16[4,256,256]{2,1,0:T(8,128)(2,1)S(1)} %constant_dynamic-update-slice_fusion.refs_0_), channel_id=1, source_target_pairs={{24,0},{0,8},{8,16},{16,24},{25,1},{1,9},{9,17},{17,25},{26,2},{2,... | collective-permute-start | bytes 1572872 | tf_op jit(solution)/shard_map/cond/branch_0_fun/ppermute | solution.py:26
  27.0 15.1 %collective-permute-start.9 = (bf16[4,256,256]{2,1,0:T(8,128)(2,1)S(1)}, bf16[4,256,256]{2,1,0:T(8,128)(2,1)S(1)}, u32[]{:S(2)}, u32[]{:S(2)}) collective-permute-start(bf16[4,256,256]{2,1,0:T(8,128)(2,1)S(1)} %constant_dynamic-update-slice_fusion.4.refs_1_), channel_id=1, source_target_pairs={{8,0},{16,8},{24,16},{0,24},{9,1},{17,9},{25,17},{1,25},{10,2},{18... | collective-permute-start | bytes 1572872 | tf_op jit(solution)/shard_map/cond/branch_0_fun/ppermute | solution.py:26
  29.7 12.4 %collective-permute-start.11 = (bf16[4,256,256]{2,1,0:T(8,128)(2,1)S(1)}, bf16[4,256,256]{2,1,0:T(8,128)(2,1)S(1)}, u32[]{:S(2)}, u32[]{:S(2)}) collective-permute-start(bf16[4,256,256]{2,1,0:T(8,128)(2,1)S(1)} %collective-permute-done.7.refs_2_), channel_id=1, source_target_pairs={{8,0},{16,8},{24,16},{0,24},{9,1},{17,9},{25,17},{1,25},{10,2},{18... | collective-permute-start | bytes 1572872 | tf_op jit(solution)/shard_map/cond/branch_0_fun/ppermute | solution.py:26
  36.1 11.5 %collective-permute-start.12 = (bf16[4,256,256]{2,1,0:T(8,128)(2,1)S(1)}, bf16[4,256,256]{2,1,0:T(8,128)(2,1)S(1)}, u32[]{:S(2)}, u32[]{:S(2)}) collective-permute-start(bf16[4,256,256]{2,1,0:T(8,128)(2,1)S(1)} %collective-permute-done.10.refs_5_), channel_id=1, source_target_pairs={{24,0},{0,8},{8,16},{16,24},{25,1},{1,9},{9,17},{17,25},{26,2},{2,... | collective-permute-start | bytes 1572872 | tf_op jit(solution)/shard_map/cond/branch_0_fun/ppermute | solution.py:26

commit v3 on v2

--- a/solution.py
+++ b/solution.py
@@ -181,8 +181,8 @@
 
     grouped = lax.cond(
         lax.axis_index("c") == 0,
+        functools.partial(run, gather_z_then_y),
         functools.partial(run, gather_y_then_z),
-        functools.partial(run, gather_z_then_y),
         own, hidden, norm_gain, place, owner, lengths, cosine, sine,
     )
     landed = lax.all_to_all(grouped, ("x", "c"), split_axis=0, concat_axis=0, tiled=True)

time: 109 us -> 108 us (level)
  waiting for transfers between devices: 25.7 us -> 16.2 us
  starting transfers between devices: 19.8 us -> 25.5 us
  blocking collectives: 43.3 us -> 46.6 us
    ppermute x6 -> x3, waiting for transfers between devices: 15.9 us -> 1.68 us  [from_y(): return lax.ppermute(value, 'y', [((s + step) % NY, s) for s in range(NY)])]
    ppermute x7 -> x14, starting transfers between devices: 12.8 us -> 20.8 us  [from_z(): return lax.ppermute(value, 'z', [((s + step) % NZ, s) for s in range(NZ)])]
    ppermute x7 -> x14, waiting for transfers between devices: 9.79 us -> 14.6 us  [from_z(): return lax.ppermute(value, 'z', [((s + step) % NZ, s) for s in range(NZ)])]
    all_to_all x1, blocking collectives: 22.7 us -> 26.2 us  [shards(): lax.all_to_all(grouped, ('x', 'c'), split_axis=0, concat_axis=0, tiled=True)]
    ppermute x6 -> x3, starting transfers between devices: 7.02 us -> 4.68 us  [from_y(): return lax.ppermute(value, 'y', [((s + step) % NY, s) for s in range(NY)])]
  transfers between devices with their start and end apart: 13 -> 17, of which waited for: 7 -> 10; matrix products, arithmetic and copies ran while one was open for 2% -> 2% of each run, Pallas kernels for 0% -> 0%
where the time goes in v3:
time: 108 us
  blocking collectives  46.6 us (43%)
  starting transfers between devices  25.5 us (24%)
  Pallas kernels  17.3 us (16%)
  waiting for transfers between devices  16.2 us (15%)
  local copies, waits for them, and re-layouts  1.71 us (2%)
    all_to_all x1, blocking collectives, shards(): lax.all_to_all(grouped, ('x', 'c'), split_axis=0, concat_axis=0, tiled=True)  26.2 us
    ppermute x14, starting transfers between devices, from_z(): return lax.ppermute(value, 'z', [((s + step) % NZ, s) for s in range(NZ)])  20.8 us
    all_to_all x1, blocking collectives, run(): lax.all_to_all(by_target, ('z', 'y'), split_axis=0, concat_axis=0, tiled=...  20.4 us
    pallas_call x1, Pallas kernels, project(): pl.pallas_call(functools.partial(project_kernel, [m for _, m in pieces]),...  16.4 us
    ppermute x14, waiting for transfers between devices, from_z(): return lax.ppermute(value, 'z', [((s + step) % NZ, s) for s in range(NZ)])  14.6 us
    ppermute x3, starting transfers between devices, from_y(): return lax.ppermute(value, 'y', [((s + step) % NY, s) for s in range(NY)])  4.68 us
  transfers between devices with their start and end apart: 17, of which 10 were waited for; matrix products, arithmetic and copies ran while one was open for 2% of the time, Pallas kernels for 0%

profile of v3, /device:TPU:1, one launch (start us, length us, event | category | flops | bytes accessed | tf_op | source)
XLA Modules:
  0.0 107.8 jit_solution(9182531755202236752)
XLA Ops:
  0.3 80.4 %conditional.1 = (bf16[32,48,256]{2,1,0:T(8,128)(2,1)S(1)}) conditional(s32[]{:T(128)} %convert_element_type.3, (bf16[8192]{0:T(1024)(128)(2,1)}, bf16[1,256,256]{2,1,0:T(8,128)(2,1)}, s32[2]{0:T(128)S(1)}, s32[32]{0:T(128)}, s32[32]{0:T(128)}, /*index=5*/bf16[32,48,8192]{2,1,0:T(8,128)(2,1)}, f32[48,128]{1,0:T(8,128)S(1)}, ...), branch_computations={%region_0.0_spmd, %region_1.0_spmd} | conditional | flops 6442450944 | bytes 45122064 | solution.py:182
  0.3 3.6 %collective-permute-start = (bf16[1,256,256]{2,1,0:T(8,128)(2,1)}, bf16[1,256,256]{2,1,0:T(8,128)(2,1)S(1)}, u32[]{:S(2)}, u32[]{:S(2)}) collective-permute-start(bf16[1,256,256]{2,1,0:T(8,128)(2,1)} %get-tuple-element.47), channel_id=1, source_target_pairs={{8,0},{16,8},{24,16},{0,24},{9,1},{17,9},{25,17},{1,25},{10,2},{18... | collective-permute-start | bytes 393224 | tf_op jit(solution)/shard_map/cond/branch_0_fun/ppermute | solution.py:26
  4.3 0.7 collective-permute-start.1
  5.0 0.9 constant_dynamic-update-slice_fusion.1
  5.9 1.7 %collective-permute-done = bf16[1,256,256]{2,1,0:T(8,128)(2,1)S(1)} collective-permute-done((bf16[1,256,256]{2,1,0:T(8,128)(2,1)}, bf16[1,256,256]{2,1,0:T(8,128)(2,1)S(1)}, u32[]{:S(2)}, u32[]{:S(2)}) %collective-permute-start) | collective-permute-done | bytes 131104 | tf_op jit(solution)/shard_map/cond/branch_0_fun/ppermute | solution.py:26
  7.6 5.7 %collective-permute-start.3 = (bf16[2,256,256]{2,1,0:T(8,128)(2,1)S(1)}, bf16[2,256,256]{2,1,0:T(8,128)(2,1)S(1)}, u32[]{:S(2)}, u32[]{:S(2)}) collective-permute-start(bf16[2,256,256]{2,1,0:T(8,128)(2,1)S(1)} %constant_dynamic-update-slice_fusion.refs_0_), channel_id=1, source_target_pairs={{32,0},{64,32},{96,64},{128,96},{160,128},{192,160},{224,192},{0,2... | collective-permute-start | bytes 786440 | tf_op jit(solution)/shard_map/cond/branch_0_fun/ppermute | solution.py:22
  13.4 0.9 collective-permute-start.4
  14.3 2.8 %collective-permute-start.5 = (bf16[2,256,256]{2,1,0:T(8,128)(2,1)S(1)}, bf16[2,256,256]{2,1,0:T(8,128)(2,1)S(1)}, u32[]{:S(2)}, u32[]{:S(2)}) collective-permute-start(bf16[2,256,256]{2,1,0:T(8,128)(2,1)S(1)} %constant_dynamic-update-slice_fusion.2.refs_1_), channel_id=1, source_target_pairs={{32,0},{64,32},{96,64},{128,96},{160,128},{192,160},{224,192},{0,2... | collective-permute-start | bytes 786440 | tf_op jit(solution)/shard_map/cond/branch_0_fun/ppermute | solution.py:22
  17.1 2.7 %collective-permute-start.7 = (bf16[2,256,256]{2,1,0:T(8,128)(2,1)S(1)}, bf16[2,256,256]{2,1,0:T(8,128)(2,1)S(1)}, u32[]{:S(2)}, u32[]{:S(2)}) collective-permute-start(bf16[2,256,256]{2,1,0:T(8,128)(2,1)S(1)} %collective-permute-done.3.refs_2_), channel_id=1, source_target_pairs={{32,0},{64,32},{96,64},{128,96},{160,128},{192,160},{224,192},{0,2... | collective-permute-start | bytes 786440 | tf_op jit(solution)/shard_map/cond/branch_0_fun/ppermute | solution.py:22
  19.7 1.5 %collective-permute-done.6.refs_5_ = bf16[2,256,256]{2,1,0:T(8,128)(2,1)S(1)} collective-permute-done((bf16[2,256,256]{2,1,0:T(8,128)(2,1)S(1)}, bf16[2,256,256]{2,1,0:T(8,128)(2,1)S(1)}, u32[]{:S(2)}, u32[]{:S(2)}) %collective-permute-start.6) | collective-permute-done | bytes 262176 | tf_op jit(solution)/shard_map/cond/branch_0_fun/ppermute | solution.py:22
  21.2 2.8 %collective-permute-done.4.refs_3_ = bf16[2,256,256]{2,1,0:T(8,128)(2,1)S(1)} collective-permute-done((bf16[2,256,256]{2,1,0:T(8,128)(2,1)S(1)}, bf16[2,256,256]{2,1,0:T(8,128)(2,1)S(1)}, u32[]{:S(2)}, u32[]{:S(2)}) %collective-permute-start.4) | collective-permute-done | bytes 262176 | tf_op jit(solution)/shard_map/cond/branch_0_fun/ppermute | solution.py:22
  24.0 2.7 %collective-permute-start.9 = (bf16[2,256,256]{2,1,0:T(8,128)(2,1)S(1)}, bf16[2,256,256]{2,1,0:T(8,128)(2,1)S(1)}, u32[]{:S(2)}, u32[]{:S(2)}) collective-permute-start(bf16[2,256,256]{2,1,0:T(8,128)(2,1)S(1)} %collective-permute-done.5.refs_4_), channel_id=1, source_target_pairs={{32,0},{64,32},{96,64},{128,96},{160,128},{192,160},{224,192},{0,2... | collective-permute-start | bytes 786440 | tf_op jit(solution)/shard_map/cond/branch_0_fun/ppermute | solution.py:22
  26.7 0.9 collective-permute-start.11
  28.2 3.7 %collective-permute-done.8.refs_7_ = bf16[2,256,256]{2,1,0:T(8,128)(2,1)S(1)} collective-permute-done((bf16[2,256,256]{2,1,0:T(8,128)(2,1)S(1)}, bf16[2,256,256]{2,1,0:T(8,128)(2,1)S(1)}, u32[]{:S(2)}, u32[]{:S(2)}) %collective-permute-start.8) | collective-permute-done | bytes 262176 | tf_op jit(solution)/shard_map/cond/branch_0_fun/ppermute | solution.py:22
  32.0 2.5 %collective-permute-start.13 = (bf16[2,256,256]{2,1,0:T(8,128)(2,1)S(1)}, bf16[2,256,256]{2,1,0:T(8,128)(2,1)S(1)}, u32[]{:S(2)}, u32[]{:S(2)}) collective-permute-start(bf16[2,256,256]{2,1,0:T(8,128)(2,1)S(1)} %collective-permute-done.9.refs_8_), channel_id=1, source_target_pairs={{32,0},{64,32},{96,64},{128,96},{160,128},{192,160},{224,192},{0,2... | collective-permute-start | bytes 786440 | tf_op jit(solution)/shard_map/cond/branch_0_fun/ppermute | solution.py:22
  34.9 2.3 %collective-permute-start.15 = (bf16[2,256,256]{2,1,0:T(8,128)(2,1)S(1)}, bf16[2,256,256]{2,1,0:T(8,128)(2,1)S(1)}, u32[]{:S(2)}, u32[]{:S(2)}) collective-permute-start(bf16[2,256,256]{2,1,0:T(8,128)(2,1)S(1)} %collective-permute-done.11.refs_10_), channel_id=1, source_target_pairs={{32,0},{64,32},{96,64},{128,96},{160,128},{192,160},{224,192},{0,2... | collective-permute-start | bytes 786440 | tf_op jit(solution)/shard_map/cond/branch_0_fun/ppermute | solution.py:22
  37.1 0.7 reshape.15.gain_ref
  37.9 0.7 collective-permute-done.12.refs_11_
  38.6 2.2 %collective-permute-done.15.refs_14_ = bf16[2,256,256]{2,1,0:T(8,128)(2,1)S(1)} collective-permute-done((bf16[2,256,256]{2,1,0:T(8,128)(2,1)S(1)}, bf16[2,256,256]{2,1,0:T(8,128)(2,1)S(1)}, u32[]{:S(2)}, u32[]{:S(2)}) %collective-permute-start.15) | collective-permute-done | bytes 262176 | tf_op jit(solution)/shard_map/cond/branch_0_fun/ppermute | solution.py:22
  40.8 3.1 %collective-permute-done.16.refs_15_ = bf16[2,256,256]{2,1,0:T(8,128)(2,1)S(1)} collective-permute-done((bf16[2,256,256]{2,1,0:T(8,128)(2,1)S(1)}, bf16[2,256,256]{2,1,0:T(8,128)(2,1)S(1)}, u32[]{:S(2)}, u32[]{:S(2)}) %collective-permute-start.16) | collective-permute-done | bytes 262176 | tf_op jit(solution)/shard_map/cond/branch_0_fun/ppermute | solution.py:22
  43.8 16.4 %project.2 = bf16[32,48,256]{2,1,0:T(8,128)(2,1)S(1)} custom-call(s32[2]{0:T(128)S(1)} %get-tuple-element.40.place_ref, s32[32]{0:T(128)} %get-tuple-element.41.slot_ref, s32[32]{0:T(128)} %get-tuple-element.42.length_ref, bf16[32,48,8192]{2,1,0:T(8,128)(2,1)} %get-tuple-element.43.hidden_ref, f32[48,128]{1,0:T(8,128)S(1)} %get-tuple-element.44.cosine_ref, ...), custom_call_target="tpu_custom_call" | custom-call | flops 6442450944 | bytes 25165824 | tf_op jit(solution)/shard_map/cond/branch_0_fun/project/pallas_call | solution.py:128
  60.2 20.4 %all_to_all.13 = bf16[32,48,256]{2,1,0:T(8,128)(2,1)S(1)} all-to-all(bf16[32,48,256]{2,1,0:T(8,128)(2,1)S(1)} %project.2), channel_id=1, replica_groups=mesh['z'=8,'y'=4,'x'=4,'c'=2] {'z','y'}, dimensions={0} | all-to-all | bytes 1572864 | tf_op jit(solution)/shard_map/cond/branch_0_fun/all_to_all | solution.py:148
  80.7 26.2 %all_to_all.15 = bf16[32,48,256]{2,1,0:T(8,128)(2,1)S(1)} all-to-all(bf16[32,48,256]{2,1,0:T(8,128)(2,1)S(1)} %get-tuple-element.61), channel_id=1, replica_groups=mesh['z'=8,'y'=4,'x'=4,'c'=2] {'x','c'}, dimensions={0} | all-to-all | bytes 1572864 | tf_op jit(solution)/shard_map/all_to_all | solution.py:188
  106.9 1.0 side_by_side.1
  (24 shorter events, 1.8 us)
Async XLA Ops:
  0.3 7.3 %collective-permute-start = (bf16[1,256,256]{2,1,0:T(8,128)(2,1)}, bf16[1,256,256]{2,1,0:T(8,128)(2,1)S(1)}, u32[]{:S(2)}, u32[]{:S(2)}) collective-permute-start(bf16[1,256,256]{2,1,0:T(8,128)(2,1)} %get-tuple-element.47), channel_id=1, source_target_pairs={{8,0},{16,8},{24,16},{0,24},{9,1},{17,9},{25,17},{1,25},{10,2},{18... | collective-permute-start | bytes 393224 | tf_op jit(solution)/shard_map/cond/branch_0_fun/ppermute | solution.py:26
  3.9 9.4 %collective-permute-start.2 = (bf16[1,256,256]{2,1,0:T(8,128)(2,1)}, bf16[1,256,256]{2,1,0:T(8,128)(2,1)S(1)}, u32[]{:S(2)}, u32[]{:S(2)}) collective-permute-start(bf16[1,256,256]{2,1,0:T(8,128)(2,1)} %get-tuple-element.47), channel_id=1, source_target_pairs={{16,0},{24,8},{0,16},{8,24},{17,1},{25,9},{1,17},{9,25},{18,2},{26... | collective-permute-start | bytes 393224 | tf_op jit(solution)/shard_map/cond/branch_0_fun/ppermute | solution.py:26
  4.3 9.0 %collective-permute-start.1 = (bf16[1,256,256]{2,1,0:T(8,128)(2,1)}, bf16[1,256,256]{2,1,0:T(8,128)(2,1)S(1)}, u32[]{:S(2)}, u32[]{:S(2)}) collective-permute-start(bf16[1,256,256]{2,1,0:T(8,128)(2,1)} %get-tuple-element.47), channel_id=1, source_target_pairs={{24,0},{0,8},{8,16},{16,24},{25,1},{1,9},{9,17},{17,25},{26,2},{2,... | collective-permute-start | bytes 393224 | tf_op jit(solution)/shard_map/cond/branch_0_fun/ppermute | solution.py:26
  7.6 9.4 %collective-permute-start.3 = (bf16[2,256,256]{2,1,0:T(8,128)(2,1)S(1)}, bf16[2,256,256]{2,1,0:T(8,128)(2,1)S(1)}, u32[]{:S(2)}, u32[]{:S(2)}) collective-permute-start(bf16[2,256,256]{2,1,0:T(8,128)(2,1)S(1)} %constant_dynamic-update-slice_fusion.refs_0_), channel_id=1, source_target_pairs={{32,0},{64,32},{96,64},{128,96},{160,128},{192,160},{224,192},{0,2... | collective-permute-start | bytes 786440 | tf_op jit(solution)/shard_map/cond/branch_0_fun/ppermute | solution.py:22
  13.3 7.9 %collective-permute-start.6 = (bf16[2,256,256]{2,1,0:T(8,128)(2,1)S(1)}, bf16[2,256,256]{2,1,0:T(8,128)(2,1)S(1)}, u32[]{:S(2)}, u32[]{:S(2)}) collective-permute-start(bf16[2,256,256]{2,1,0:T(8,128)(2,1)S(1)} %constant_dynamic-update-slice_fusion.2.refs_1_), channel_id=1, source_target_pairs={{224,0},{0,32},{32,64},{64,96},{96,128},{128,160},{160,192},{192,2... | collective-permute-start | bytes 786440 | tf_op jit(solution)/shard_map/cond/branch_0_fun/ppermute | solution.py:22
  13.4 10.6 %collective-permute-start.4 = (bf16[2,256,256]{2,1,0:T(8,128)(2,1)S(1)}, bf16[2,256,256]{2,1,0:T(8,128)(2,1)S(1)}, u32[]{:S(2)}, u32[]{:S(2)}) collective-permute-start(bf16[2,256,256]{2,1,0:T(8,128)(2,1)S(1)} %constant_dynamic-update-slice_fusion.refs_0_), channel_id=1, source_target_pairs={{224,0},{0,32},{32,64},{64,96},{96,128},{128,160},{160,192},{192,2... | collective-permute-start | bytes 786440 | tf_op jit(solution)/shard_map/cond/branch_0_fun/ppermute | solution.py:22
  14.3 9.7 %collective-permute-start.5 = (bf16[2,256,256]{2,1,0:T(8,128)(2,1)S(1)}, bf16[2,256,256]{2,1,0:T(8,128)(2,1)S(1)}, u32[]{:S(2)}, u32[]{:S(2)}) collective-permute-start(bf16[2,256,256]{2,1,0:T(8,128)(2,1)S(1)} %constant_dynamic-update-slice_fusion.2.refs_1_), channel_id=1, source_target_pairs={{32,0},{64,32},{96,64},{128,96},{160,128},{192,160},{224,192},{0,2... | collective-permute-start | bytes 786440 | tf_op jit(solution)/shard_map/cond/branch_0_fun/ppermute | solution.py:22
  17.1 9.7 %collective-permute-start.7 = (bf16[2,256,256]{2,1,0:T(8,128)(2,1)S(1)}, bf16[2,256,256]{2,1,0:T(8,128)(2,1)S(1)}, u32[]{:S(2)}, u32[]{:S(2)}) collective-permute-start(bf16[2,256,256]{2,1,0:T(8,128)(2,1)S(1)} %collective-permute-done.3.refs_2_), channel_id=1, source_target_pairs={{32,0},{64,32},{96,64},{128,96},{160,128},{192,160},{224,192},{0,2... | collective-permute-start | bytes 786440 | tf_op jit(solution)/shard_map/cond/branch_0_fun/ppermute | solution.py:22
  21.2 6.6 %collective-permute-start.10 = (bf16[2,256,256]{2,1,0:T(8,128)(2,1)S(1)}, bf16[2,256,256]{2,1,0:T(8,128)(2,1)S(1)}, u32[]{:S(2)}, u32[]{:S(2)}) collective-permute-start(bf16[2,256,256]{2,1,0:T(8,128)(2,1)S(1)} %collective-permute-done.6.refs_5_), channel_id=1, source_target_pairs={{224,0},{0,32},{32,64},{64,96},{96,128},{128,160},{160,192},{192,2... | collective-permute-start | bytes 786440 | tf_op jit(solution)/shard_map/cond/branch_0_fun/ppermute | solution.py:22
  24.0 7.9 %collective-permute-start.8 = (bf16[2,256,256]{2,1,0:T(8,128)(2,1)S(1)}, bf16[2,256,256]{2,1,0:T(8,128)(2,1)S(1)}, u32[]{:S(2)}, u32[]{:S(2)}) collective-permute-start(bf16[2,256,256]{2,1,0:T(8,128)(2,1)S(1)} %collective-permute-done.4.refs_3_), channel_id=1, source_target_pairs={{224,0},{0,32},{32,64},{64,96},{96,128},{128,160},{160,192},{192,2... | collective-permute-start | bytes 786440 | tf_op jit(solution)/shard_map/cond/branch_0_fun/ppermute | solution.py:22
  24.0 8.0 %collective-permute-start.9 = (bf16[2,256,256]{2,1,0:T(8,128)(2,1)S(1)}, bf16[2,256,256]{2,1,0:T(8,128)(2,1)S(1)}, u32[]{:S(2)}, u32[]{:S(2)}) collective-permute-start(bf16[2,256,256]{2,1,0:T(8,128)(2,1)S(1)} %collective-permute-done.5.refs_4_), channel_id=1, source_target_pairs={{32,0},{64,32},{96,64},{128,96},{160,128},{192,160},{224,192},{0,2... | collective-permute-start | bytes 786440 | tf_op jit(solution)/shard_map/cond/branch_0_fun/ppermute | solution.py:22
  26.7 8.1 %collective-permute-start.11 = (bf16[2,256,256]{2,1,0:T(8,128)(2,1)S(1)}, bf16[2,256,256]{2,1,0:T(8,128)(2,1)S(1)}, u32[]{:S(2)}, u32[]{:S(2)}) collective-permute-start(bf16[2,256,256]{2,1,0:T(8,128)(2,1)S(1)} %collective-permute-done.7.refs_6_), channel_id=1, source_target_pairs={{32,0},{64,32},{96,64},{128,96},{160,128},{192,160},{224,192},{0,2... | collective-permute-start | bytes 786440 | tf_op jit(solution)/shard_map/cond/branch_0_fun/ppermute | solution.py:22
  27.8 9.3 %collective-permute-start.14 = (bf16[2,256,256]{2,1,0:T(8,128)(2,1)S(1)}, bf16[2,256,256]{2,1,0:T(8,128)(2,1)S(1)}, u32[]{:S(2)}, u32[]{:S(2)}) collective-permute-start(bf16[2,256,256]{2,1,0:T(8,128)(2,1)S(1)} %collective-permute-done.10.refs_9_), channel_id=1, source_target_pairs={{224,0},{0,32},{32,64},{64,96},{96,128},{128,160},{160,192},{192,2... | collective-permute-start | bytes 786440 | tf_op jit(solution)/shard_map/cond/branch_0_fun/ppermute | solution.py:22
  31.9 6.7 %collective-permute-start.12 = (bf16[2,256,256]{2,1,0:T(8,128)(2,1)S(1)}, bf16[2,256,256]{2,1,0:T(8,128)(2,1)S(1)}, u32[]{:S(2)}, u32[]{:S(2)}) collective-permute-start(bf16[2,256,256]{2,1,0:T(8,128)(2,1)S(1)} %collective-permute-done.8.refs_7_), channel_id=1, source_target_pairs={{224,0},{0,32},{32,64},{64,96},{96,128},{128,160},{160,192},{192,2... | collective-permute-start | bytes 786440 | tf_op jit(solution)/shard_map/cond/branch_0_fun/ppermute | solution.py:22
  32.0 6.6 %collective-permute-start.13 = (bf16[2,256,256]{2,1,0:T(8,128)(2,1)S(1)}, bf16[2,256,256]{2,1,0:T(8,128)(2,1)S(1)}, u32[]{:S(2)}, u32[]{:S(2)}) collective-permute-start(bf16[2,256,256]{2,1,0:T(8,128)(2,1)S(1)} %collective-permute-done.9.refs_8_), channel_id=1, source_target_pairs={{32,0},{64,32},{96,64},{128,96},{160,128},{192,160},{224,192},{0,2... | collective-permute-start | bytes 786440 | tf_op jit(solution)/shard_map/cond/branch_0_fun/ppermute | solution.py:22
  34.9 5.9 %collective-permute-start.15 = (bf16[2,256,256]{2,1,0:T(8,128)(2,1)S(1)}, bf16[2,256,256]{2,1,0:T(8,128)(2,1)S(1)}, u32[]{:S(2)}, u32[]{:S(2)}) collective-permute-start(bf16[2,256,256]{2,1,0:T(8,128)(2,1)S(1)} %collective-permute-done.11.refs_10_), channel_id=1, source_target_pairs={{32,0},{64,32},{96,64},{128,96},{160,128},{192,160},{224,192},{0,2... | collective-permute-start | bytes 786440 | tf_op jit(solution)/shard_map/cond/branch_0_fun/ppermute | solution.py:22
  37.1 6.7 %collective-permute-start.16 = (bf16[2,256,256]{2,1,0:T(8,128)(2,1)S(1)}, bf16[2,256,256]{2,1,0:T(8,128)(2,1)S(1)}, u32[]{:S(2)}, u32[]{:S(2)}) collective-permute-start(bf16[2,256,256]{2,1,0:T(8,128)(2,1)S(1)} %collective-permute-done.14.refs_13_), channel_id=1, source_target_pairs={{224,0},{0,32},{32,64},{64,96},{96,128},{128,160},{160,192},{192,2... | collective-permute-start | bytes 786440 | tf_op jit(solution)/shard_map/cond/branch_0_fun/ppermute | solution.py:22
